TPU v7x, 256 devices: a whole 4x4x8 slice. The times are simulated.
256 devices in a mesh: dp: 16 (over x, z_hi), ctx: 16 (over z_lo, y, core).
Axes of the slice: x: 4, y: 4, z: 8 (z_hi: 4, z_lo: 2; z = z_hi * 2 + z_lo), core: 2. Of those that a mesh axis runs over, the one named last changes fastest.
Arguments:
- hidden_in: bfloat16 [16, 4096, 8192], P('dp', 'ctx'), may hold values from -6 to 6
- queries: bfloat16 [16, 4096, 4096], P('dp', 'ctx'), may hold values from -128 to 128
- key_projection_weight: bfloat16 [8192, 512], P('dp'), may hold values from -0.0625 to 0.0625
- value_projection_weight: bfloat16 [8192, 512], P('dp'), may hold values from -0.0625 to 0.0625
- key_projection_bias: float32 [512], replicated, may hold values from -2.5 to 2.5
- value_projection_bias: float32 [512], replicated, may hold values from -3 to 3
- block_segments: int32 [16, 32], P('dp'), may hold values from 0 to 4, never falling along the last dimension, each value on 1 to 12 neighbouring positions
Outputs:
- attended: bfloat16 [16, 4096, 4096], P('dp', 'ctx')
Inputs may be any that keep to these rules, and one draw needn't show every extreme that they name: `block_segments`: each row starts with segment 0 and never falls; every one of the 5 segments spans 1 to 12 blocks.
All inputs are finite; a program needn't handle non-finite values.
Results may differ from a plain program's by a relative error of at most 0.0079.
Values may be sent and summed in bfloat16 or wider, within the bound.
A program may use at most 128 MiB of HBM per device.

v0:
```python
import math

import jax
import jax.numpy as jnp
from jax import lax
from jax.sharding import PartitionSpec as P

HEAD_SIZE = 128
KEY_VALUE_HEADS = 4
BLK = 128


rope_base = 1000000.0


def passed_along(x, axis, by):
    count = lax.axis_size(axis)
    pairs = [(i, i + by) for i in range(count) if 0 <= i + by < count]
    return lax.ppermute(x, axis, pairs)


def rotary_rotate(head_vecs, token_positions):
    half_dim = head_vecs.shape[-1] // 2
    frequency = rope_base ** (
        -(jnp.arange(half_dim, dtype=jnp.float32) * 2.0 / head_vecs.shape[-1])
    )
    angles = token_positions.astype(jnp.float32)[:, None] * frequency[None, :]
    cos_part = jnp.cos(angles)[:, None, :]
    sine_part = jnp.sin(angles)[:, None, :]
    first_half = head_vecs[..., :half_dim]
    second_half = head_vecs[..., half_dim:]
    return jnp.concatenate(
        [
            first_half * cos_part - second_half * sine_part,
            second_half * cos_part + first_half * sine_part,
        ],
        axis=-1,
    )


def body(
    hidden_in,
    queries,
    key_projection_weight,
    value_projection_weight,
    key_projection_bias,
    value_projection_bias,
    block_segments,
):
    tokens = hidden_in[0]
    number_of_rows = tokens.shape[0]
    kv_width = key_projection_weight.shape[1]
    query_head_count = queries.shape[2] // HEAD_SIZE
    group_width = query_head_count // KEY_VALUE_HEADS
    ctx_size = lax.axis_size("ctx")
    my_index = lax.axis_index("ctx")
    key_projected_rows = jnp.dot(
        tokens,
        lax.all_gather(key_projection_weight, "dp", axis=0, tiled=True),
        preferred_element_type=jnp.float32,
    )
    value_proj = jnp.dot(
        tokens,
        lax.all_gather(value_projection_weight, "dp", axis=0, tiled=True),
        preferred_element_type=jnp.float32,
    )
    token_positions = my_index * number_of_rows + jnp.arange(number_of_rows, dtype=jnp.int32)
    key_row_values = rotary_rotate(
        (key_projected_rows + key_projection_bias).reshape(
            number_of_rows, KEY_VALUE_HEADS, HEAD_SIZE
        ),
        token_positions,
    )
    key_row_values = key_row_values.astype(jnp.bfloat16).reshape(number_of_rows, kv_width)
    value_row_values = (value_proj + value_projection_bias).astype(jnp.bfloat16)
    stacked = jnp.stack([key_row_values, value_row_values])
    segment_tokens = jnp.repeat(block_segments[0], BLK)
    query_seg = lax.dynamic_slice_in_dim(segment_tokens, my_index * number_of_rows, number_of_rows)
    query_head_values = queries[0].reshape(number_of_rows, KEY_VALUE_HEADS, group_width, HEAD_SIZE)
    score_scale = 1.0 / math.sqrt(HEAD_SIZE)

    def attend(carried, key_value_portion, first_row, usable):
        token_length = key_value_portion.shape[1]
        key_pos = first_row + jnp.arange(token_length, dtype=jnp.int32)
        key_seg = lax.dynamic_slice_in_dim(segment_tokens, first_row, token_length)
        allowed = (key_pos[None, :] <= token_positions[:, None]) & (
            (key_seg[None, :] == query_seg[:, None]) | (key_seg[None, :] == 0)
        )
        allowed = allowed & usable

        def update(current):
            row_peak, row_total, weighted = current
            key_portion = key_value_portion[0].reshape(token_length, KEY_VALUE_HEADS, HEAD_SIZE)
            value_portion = key_value_portion[1].reshape(token_length, KEY_VALUE_HEADS, HEAD_SIZE)
            scores = (
                jnp.einsum(
                    "tkgd,skd->tkgs",
                    query_head_values,
                    key_portion,
                    preferred_element_type=jnp.float32,
                )
                * score_scale
            )
            scores = jnp.where(allowed[:, None, None, :], scores, -jnp.inf)
            new_peak = jnp.maximum(row_peak, jnp.max(scores, axis=-1))
            factor = jnp.exp(row_peak - new_peak)
            expd = jnp.exp(scores - new_peak[..., None])
            row_total = row_total * factor + jnp.sum(expd, axis=-1)
            weighted = weighted * factor[..., None] + jnp.einsum(
                "tkgs,skd->tkgd",
                expd.astype(jnp.bfloat16),
                value_portion,
                preferred_element_type=jnp.float32,
            )
            return (new_peak, row_total, weighted)

        return lax.cond(jnp.any(allowed), update, lambda current: current, carried)

    initial = (
        jnp.full((number_of_rows, KEY_VALUE_HEADS, group_width), -1e30, jnp.float32),
        jnp.zeros((number_of_rows, KEY_VALUE_HEADS, group_width), jnp.float32),
        jnp.zeros((number_of_rows, KEY_VALUE_HEADS, group_width, HEAD_SIZE), jnp.float32),
    )
    carried = attend(initial, stacked, my_index * number_of_rows, True)

    def advance(hop_index, loop_state):
        current, travelling = loop_state
        travelling = passed_along(travelling, "ctx", 1)
        current = attend(
            current, travelling, (my_index - hop_index) * number_of_rows, my_index >= hop_index
        )
        return (current, travelling)

    carried, travelling = lax.fori_loop(1, ctx_size, advance, (carried, stacked))
    row_peak, row_total, weighted = carried
    attended = (weighted / row_total[..., None]).astype(jnp.bfloat16)
    return attended.reshape(1, number_of_rows, query_head_count * HEAD_SIZE)


def solution(mesh):
    placed = (
        P("dp", "ctx", None),
        P("dp", "ctx", None),
        P("dp", None),
        P("dp", None),
        P(),
        P(),
        P("dp", None),
    )
    return jax.shard_map(
        body, mesh=mesh, in_specs=placed, out_specs=P("dp", "ctx", None), check_vma=False
    )
```

profile of v0, /device:TPU:61, one launch (start us, length us, event | category | flops | bytes accessed | tf_op | source)
XLA Modules:
  0.0 609.1 jit_solution(1849066501224094741)
XLA Ops:
  17.3 111.6 %all-gather.3.cloned.1.call-done = bf16[8192,512]{1,0:T(8,128)(2,1)} async-done(((bf16[512,512]{1,0:T(8,128)(2,1)}), bf16[8192,512]{1,0:T(8,128)(2,1)}) %all-gather.3.cloned.1.call-update) | async-done | bytes 8388624 | tf_op jit(solution)/shard_map/all_gather | solution.py:59
  128.9 7.0 %fusion.36 = f32[256,512]{1,0:T(8,128)S(1)} fusion(bf16[8192,512]{1,0:T(8,128)(2,1)} %all-gather.3.cloned.1.call-done, bf16[1,256,8192]{2,1,0:T(8,128)(2,1)} %param.13, f32[512]{0:T(512)S(1)} %copy-done.3), kind=kOutput, calls=%fused_computation.44 | convolution fusion | flops 2147614720 | bytes 13109248 | tf_op jit(solution)/shard_map/dot_general | solution.py:57
  137.0 109.2 %all-gather.5.cloned.1.call-done = bf16[8192,512]{1,0:T(8,128)(2,1)} async-done(((bf16[512,512]{1,0:T(8,128)(2,1)}), bf16[8192,512]{1,0:T(8,128)(2,1)}) %all-gather.5.cloned.1.call-update) | async-done | bytes 8388624 | tf_op jit(solution)/shard_map/all_gather | solution.py:64
  246.2 7.0 %fusion.42 = bf16[256,512]{1,0:T(8,128)(2,1)S(1)} fusion(bf16[8192,512]{1,0:T(8,128)(2,1)} %all-gather.5.cloned.1.call-done, bf16[1,256,8192]{2,1,0:T(8,128)(2,1)} %param.13, f32[512]{0:T(512)S(1)} %copy-done.4), kind=kOutput, calls=%fused_computation.46 | convolution fusion | flops 2147745792 | bytes 12847104 | tf_op jit(solution)/shard_map/dot_general | solution.py:62
  254.3 16.2 %conditional.2 = (f32[256,4,8]{0,2,1:T(8,128)}, f32[256,4,8]{0,2,1:T(8,128)S(1)}, f32[256,4,8,128]{3,0,2,1:T(8,128)}) conditional(s32[]{:T(128)} %convert_element_type.42, () %tuple.34, (pred[256,256]{0,1:T(8,128)(4,1)S(1)}, bf16[256,4,128]{2,0,1:T(8,128)(2,1)S(1)}, bf16[256,4,8,128]{0,3,2,1:T(8,128)(2,1)}, bf16[256,512]{1,0:T(8,128)(2,1)S(1)}) %tuple.86), branch_computations={%region_1.0_spmd, %region_2.5_spmd} | conditional | flops 1097891840 | bytes 66617396 | solution.py:117
  263.8 6.7 %bitcast_add_fusion = f32[256,4,8,128]{3,0,2,1:T(8,128)} fusion(f32[256,4,8]{0,2,1:T(8,128)S(1)} %get-tuple-element.288, f32[4,256,256,8]{2,1,3,0:T(8,128)} %copy-done.1, f32[256,4,8]{0,2,1:T(8,128)} %get-tuple-element.398, pred[256,256]{0,1:T(8,128)(4,1)S(1)} %get-tuple-element.194, bf16[256,4,128,1]{2,1,0,3:T(4,128)(2,1)S(1)} %bitcast.74), kind=kOutput, calls=%fused_computation.7 | convolution fusion | flops 546308096 | bytes 12976128 | tf_op jit(solution)/shard_map/cond/branch_1_fun/tkgs,skd->tkgd/dot_general | solution.py:109
  270.5 322.1 %while.20 = (s32[]{:T(128)}, f32[256,4,8]{0,2,1:T(8,128)}, f32[256,4,8]{0,2,1:T(8,128)S(1)}, f32[256,4,8,128]{3,0,2,1:T(8,128)}, bf16[2,256,512]{1,2,0:T(8,128)(...) while((s32[]{:T(128)}, f32[256,4,8]{0,2,1:T(8,128)}, ...), condition=%wide.region_11.12_spmd.clone, body=%wide.region_5.11_spmd.clone.sunk | while | flops 1099318016 | bytes 41165672 | solution.py:134
  274.4 11.8 %conditional.5 = ((f32[256,4,8]{0,2,1:T(8,128)}, f32[256,4,8]{0,2,1:T(8,128)S(1)}, f32[256,4,8,128]{3,0,2,1:T(8,128)})) conditional(s32[]{:T(128)} %convert_element_type.62, (f32[256,4,8]{0,2,1:T(8,128)}, f32[256,4,8]{0,2,1:T(8,128)S(1)}, f32[256,4,8,128]{3,0,2,1:T(8,128)}) %tuple.71, (pred[256,256]{0,1:T(8,128)(4,1)S(1)}, ...), branch_computations={%region_7.7_spmd, %region_8.10_spmd} | conditional | flops 1098924032 | bytes 37945376 | solution.py:117
  279.8 6.4 %bitcast_add_fusion.1 = f32[256,4,8,128]{3,0,2,1:T(8,128)} fusion(f32[256,4,8,128]{3,0,2,1:T(8,128)} %get-tuple-element.203, f32[256,4,8]{0,2,1:T(8,128)S(1)} %get-tuple-element.291, bf16[256,4,128,1]{0,2,3,1:T(8,128)(2,1)S(1)} %bitcast.69, f32[4,256,256,8]{2,1,3,0:T(8,128)S(1)} %get-tuple-element.303, f32[256,4,8]{0,2,1:T(8,128)S(1)} %max.2, ...), kind=kOutput, calls=%fused_computation.26 | convolution fusion | flops 547356672 | bytes 17170432 | tf_op jit(solution)/shard_map/while/body/eval_jaxpr/cond/branch_1_fun/tkgs,skd->tkgd/dot_general | solution.py:109
  289.1 7.6 %collective-permute-done = bf16[2,256,512]{1,2,0:T(8,128)(2,1)S(1)} collective-permute-done((bf16[2,256,512]{1,2,0:T(8,128)(2,1)S(1)}, bf16[2,256,512]{1,2,0:T(8,128)(2,1)S(1)}, u32[]{:S(2)}, u32[]{:S(2)}) %collective-permute-start) | collective-permute-done | bytes 524320 | tf_op jit(solution)/shard_map/while/body/eval_jaxpr/ppermute | solution.py:19
  296.8 11.8 %conditional.5 = ((f32[256,4,8]{0,2,1:T(8,128)}, f32[256,4,8]{0,2,1:T(8,128)S(1)}, f32[256,4,8,128]{3,0,2,1:T(8,128)})) conditional(s32[]{:T(128)} %convert_element_type.62, (f32[256,4,8]{0,2,1:T(8,128)}, f32[256,4,8]{0,2,1:T(8,128)S(1)}, f32[256,4,8,128]{3,0,2,1:T(8,128)}) %tuple.71, (pred[256,256]{0,1:T(8,128)(4,1)S(1)}, ...), branch_computations={%region_7.7_spmd, %region_8.10_spmd} | conditional | flops 1098924032 | bytes 37945376 | solution.py:117
  302.2 6.4 %bitcast_add_fusion.1 = f32[256,4,8,128]{3,0,2,1:T(8,128)} fusion(f32[256,4,8,128]{3,0,2,1:T(8,128)} %get-tuple-element.203, f32[256,4,8]{0,2,1:T(8,128)S(1)} %get-tuple-element.291, bf16[256,4,128,1]{0,2,3,1:T(8,128)(2,1)S(1)} %bitcast.69, f32[4,256,256,8]{2,1,3,0:T(8,128)S(1)} %get-tuple-element.303, f32[256,4,8]{0,2,1:T(8,128)S(1)} %max.2, ...), kind=kOutput, calls=%fused_computation.26 | convolution fusion | flops 547356672 | bytes 17170432 | tf_op jit(solution)/shard_map/while/body/eval_jaxpr/cond/branch_1_fun/tkgs,skd->tkgd/dot_general | solution.py:109
  311.5 7.6 %collective-permute-done = bf16[2,256,512]{1,2,0:T(8,128)(2,1)S(1)} collective-permute-done((bf16[2,256,512]{1,2,0:T(8,128)(2,1)S(1)}, bf16[2,256,512]{1,2,0:T(8,128)(2,1)S(1)}, u32[]{:S(2)}, u32[]{:S(2)}) %collective-permute-start) | collective-permute-done | bytes 524320 | tf_op jit(solution)/shard_map/while/body/eval_jaxpr/ppermute | solution.py:19
  319.2 11.8 %conditional.5 = ((f32[256,4,8]{0,2,1:T(8,128)}, f32[256,4,8]{0,2,1:T(8,128)S(1)}, f32[256,4,8,128]{3,0,2,1:T(8,128)})) conditional(s32[]{:T(128)} %convert_element_type.62, (f32[256,4,8]{0,2,1:T(8,128)}, f32[256,4,8]{0,2,1:T(8,128)S(1)}, f32[256,4,8,128]{3,0,2,1:T(8,128)}) %tuple.71, (pred[256,256]{0,1:T(8,128)(4,1)S(1)}, ...), branch_computations={%region_7.7_spmd, %region_8.10_spmd} | conditional | flops 1098924032 | bytes 37945376 | solution.py:117
  333.9 7.6 %collective-permute-done = bf16[2,256,512]{1,2,0:T(8,128)(2,1)S(1)} collective-permute-done((bf16[2,256,512]{1,2,0:T(8,128)(2,1)S(1)}, bf16[2,256,512]{1,2,0:T(8,128)(2,1)S(1)}, u32[]{:S(2)}, u32[]{:S(2)}) %collective-permute-start) | collective-permute-done | bytes 524320 | tf_op jit(solution)/shard_map/while/body/eval_jaxpr/ppermute | solution.py:19
  341.6 11.8 %conditional.5 = ((f32[256,4,8]{0,2,1:T(8,128)}, f32[256,4,8]{0,2,1:T(8,128)S(1)}, f32[256,4,8,128]{3,0,2,1:T(8,128)})) conditional(s32[]{:T(128)} %convert_element_type.62, (f32[256,4,8]{0,2,1:T(8,128)}, f32[256,4,8]{0,2,1:T(8,128)S(1)}, f32[256,4,8,128]{3,0,2,1:T(8,128)}) %tuple.71, (pred[256,256]{0,1:T(8,128)(4,1)S(1)}, ...), branch_computations={%region_7.7_spmd, %region_8.10_spmd} | conditional | flops 1098924032 | bytes 37945376 | solution.py:117
  347.0 6.4 %bitcast_add_fusion.1 = f32[256,4,8,128]{3,0,2,1:T(8,128)} fusion(f32[256,4,8,128]{3,0,2,1:T(8,128)} %get-tuple-element.203, f32[256,4,8]{0,2,1:T(8,128)S(1)} %get-tuple-element.291, bf16[256,4,128,1]{0,2,3,1:T(8,128)(2,1)S(1)} %bitcast.69, f32[4,256,256,8]{2,1,3,0:T(8,128)S(1)} %get-tuple-element.303, f32[256,4,8]{0,2,1:T(8,128)S(1)} %max.2, ...), kind=kOutput, calls=%fused_computation.26 | convolution fusion | flops 547356672 | bytes 17170432 | tf_op jit(solution)/shard_map/while/body/eval_jaxpr/cond/branch_1_fun/tkgs,skd->tkgd/dot_general | solution.py:109
  356.3 7.6 %collective-permute-done = bf16[2,256,512]{1,2,0:T(8,128)(2,1)S(1)} collective-permute-done((bf16[2,256,512]{1,2,0:T(8,128)(2,1)S(1)}, bf16[2,256,512]{1,2,0:T(8,128)(2,1)S(1)}, u32[]{:S(2)}, u32[]{:S(2)}) %collective-permute-start) | collective-permute-done | bytes 524320 | tf_op jit(solution)/shard_map/while/body/eval_jaxpr/ppermute | solution.py:19
  364.0 11.8 %conditional.5 = ((f32[256,4,8]{0,2,1:T(8,128)}, f32[256,4,8]{0,2,1:T(8,128)S(1)}, f32[256,4,8,128]{3,0,2,1:T(8,128)})) conditional(s32[]{:T(128)} %convert_element_type.62, (f32[256,4,8]{0,2,1:T(8,128)}, f32[256,4,8]{0,2,1:T(8,128)S(1)}, f32[256,4,8,128]{3,0,2,1:T(8,128)}) %tuple.71, (pred[256,256]{0,1:T(8,128)(4,1)S(1)}, ...), branch_computations={%region_7.7_spmd, %region_8.10_spmd} | conditional | flops 1098924032 | bytes 37945376 | solution.py:117
  388.0 7.6 %collective-permute-done = bf16[2,256,512]{1,2,0:T(8,128)(2,1)S(1)} collective-permute-done((bf16[2,256,512]{1,2,0:T(8,128)(2,1)S(1)}, bf16[2,256,512]{1,2,0:T(8,128)(2,1)S(1)}, u32[]{:S(2)}, u32[]{:S(2)}) %collective-permute-start) | collective-permute-done | bytes 524320 | tf_op jit(solution)/shard_map/while/body/eval_jaxpr/ppermute | solution.py:19
  398.6 7.6 %collective-permute-done = bf16[2,256,512]{1,2,0:T(8,128)(2,1)S(1)} collective-permute-done((bf16[2,256,512]{1,2,0:T(8,128)(2,1)S(1)}, bf16[2,256,512]{1,2,0:T(8,128)(2,1)S(1)}, u32[]{:S(2)}, u32[]{:S(2)}) %collective-permute-start) | collective-permute-done | bytes 524320 | tf_op jit(solution)/shard_map/while/body/eval_jaxpr/ppermute | solution.py:19
  409.1 7.6 %collective-permute-done = bf16[2,256,512]{1,2,0:T(8,128)(2,1)S(1)} collective-permute-done((bf16[2,256,512]{1,2,0:T(8,128)(2,1)S(1)}, bf16[2,256,512]{1,2,0:T(8,128)(2,1)S(1)}, u32[]{:S(2)}, u32[]{:S(2)}) %collective-permute-start) | collective-permute-done | bytes 524320 | tf_op jit(solution)/shard_map/while/body/eval_jaxpr/ppermute | solution.py:19
  419.7 7.6 %collective-permute-done = bf16[2,256,512]{1,2,0:T(8,128)(2,1)S(1)} collective-permute-done((bf16[2,256,512]{1,2,0:T(8,128)(2,1)S(1)}, bf16[2,256,512]{1,2,0:T(8,128)(2,1)S(1)}, u32[]{:S(2)}, u32[]{:S(2)}) %collective-permute-start) | collective-permute-done | bytes 524320 | tf_op jit(solution)/shard_map/while/body/eval_jaxpr/ppermute | solution.py:19
  430.2 76.9 %collective-permute-done = bf16[2,256,512]{1,2,0:T(8,128)(2,1)S(1)} collective-permute-done((bf16[2,256,512]{1,2,0:T(8,128)(2,1)S(1)}, bf16[2,256,512]{1,2,0:T(8,128)(2,1)S(1)}, u32[]{:S(2)}, u32[]{:S(2)}) %collective-permute-start) | collective-permute-done | bytes 524320 | tf_op jit(solution)/shard_map/while/body/eval_jaxpr/ppermute | solution.py:19
  507.2 11.8 %conditional.5 = ((f32[256,4,8]{0,2,1:T(8,128)}, f32[256,4,8]{0,2,1:T(8,128)S(1)}, f32[256,4,8,128]{3,0,2,1:T(8,128)})) conditional(s32[]{:T(128)} %convert_element_type.62, (f32[256,4,8]{0,2,1:T(8,128)}, f32[256,4,8]{0,2,1:T(8,128)S(1)}, f32[256,4,8,128]{3,0,2,1:T(8,128)}) %tuple.71, (pred[256,256]{0,1:T(8,128)(4,1)S(1)}, ...), branch_computations={%region_7.7_spmd, %region_8.10_spmd} | conditional | flops 1098924032 | bytes 37945376 | solution.py:117
  521.9 9.7 %collective-permute-done = bf16[2,256,512]{1,2,0:T(8,128)(2,1)S(1)} collective-permute-done((bf16[2,256,512]{1,2,0:T(8,128)(2,1)S(1)}, bf16[2,256,512]{1,2,0:T(8,128)(2,1)S(1)}, u32[]{:S(2)}, u32[]{:S(2)}) %collective-permute-start) | collective-permute-done | bytes 524320 | tf_op jit(solution)/shard_map/while/body/eval_jaxpr/ppermute | solution.py:19
  531.7 11.8 %conditional.5 = ((f32[256,4,8]{0,2,1:T(8,128)}, f32[256,4,8]{0,2,1:T(8,128)S(1)}, f32[256,4,8,128]{3,0,2,1:T(8,128)})) conditional(s32[]{:T(128)} %convert_element_type.62, (f32[256,4,8]{0,2,1:T(8,128)}, f32[256,4,8]{0,2,1:T(8,128)S(1)}, f32[256,4,8,128]{3,0,2,1:T(8,128)}) %tuple.71, (pred[256,256]{0,1:T(8,128)(4,1)S(1)}, ...), branch_computations={%region_7.7_spmd, %region_8.10_spmd} | conditional | flops 1098924032 | bytes 37945376 | solution.py:117
  537.2 6.4 %bitcast_add_fusion.1 = f32[256,4,8,128]{3,0,2,1:T(8,128)} fusion(f32[256,4,8,128]{3,0,2,1:T(8,128)} %get-tuple-element.203, f32[256,4,8]{0,2,1:T(8,128)S(1)} %get-tuple-element.291, bf16[256,4,128,1]{0,2,3,1:T(8,128)(2,1)S(1)} %bitcast.69, f32[4,256,256,8]{2,1,3,0:T(8,128)S(1)} %get-tuple-element.303, f32[256,4,8]{0,2,1:T(8,128)S(1)} %max.2, ...), kind=kOutput, calls=%fused_computation.26 | convolution fusion | flops 547356672 | bytes 17170432 | tf_op jit(solution)/shard_map/while/body/eval_jaxpr/cond/branch_1_fun/tkgs,skd->tkgd/dot_general | solution.py:109
  546.4 9.7 %collective-permute-done = bf16[2,256,512]{1,2,0:T(8,128)(2,1)S(1)} collective-permute-done((bf16[2,256,512]{1,2,0:T(8,128)(2,1)S(1)}, bf16[2,256,512]{1,2,0:T(8,128)(2,1)S(1)}, u32[]{:S(2)}, u32[]{:S(2)}) %collective-permute-start) | collective-permute-done | bytes 524320 | tf_op jit(solution)/shard_map/while/body/eval_jaxpr/ppermute | solution.py:19
  556.2 11.8 %conditional.5 = ((f32[256,4,8]{0,2,1:T(8,128)}, f32[256,4,8]{0,2,1:T(8,128)S(1)}, f32[256,4,8,128]{3,0,2,1:T(8,128)})) conditional(s32[]{:T(128)} %convert_element_type.62, (f32[256,4,8]{0,2,1:T(8,128)}, f32[256,4,8]{0,2,1:T(8,128)S(1)}, f32[256,4,8,128]{3,0,2,1:T(8,128)}) %tuple.71, (pred[256,256]{0,1:T(8,128)(4,1)S(1)}, ...), branch_computations={%region_7.7_spmd, %region_8.10_spmd} | conditional | flops 1098924032 | bytes 37945376 | solution.py:117
  571.0 9.7 %collective-permute-done = bf16[2,256,512]{1,2,0:T(8,128)(2,1)S(1)} collective-permute-done((bf16[2,256,512]{1,2,0:T(8,128)(2,1)S(1)}, bf16[2,256,512]{1,2,0:T(8,128)(2,1)S(1)}, u32[]{:S(2)}, u32[]{:S(2)}) %collective-permute-start) | collective-permute-done | bytes 524320 | tf_op jit(solution)/shard_map/while/body/eval_jaxpr/ppermute | solution.py:19
  580.7 11.8 %conditional.5 = ((f32[256,4,8]{0,2,1:T(8,128)}, f32[256,4,8]{0,2,1:T(8,128)S(1)}, f32[256,4,8,128]{3,0,2,1:T(8,128)})) conditional(s32[]{:T(128)} %convert_element_type.62, (f32[256,4,8]{0,2,1:T(8,128)}, f32[256,4,8]{0,2,1:T(8,128)S(1)}, f32[256,4,8,128]{3,0,2,1:T(8,128)}) %tuple.71, (pred[256,256]{0,1:T(8,128)(4,1)S(1)}, ...), branch_computations={%region_7.7_spmd, %region_8.10_spmd} | conditional | flops 1098924032 | bytes 37945376 | solution.py:117
  (196 shorter events, 150.2 us)
Async XLA Ops:
  6.5 1.5 copy-start
  6.5 122.3 %copy-start.3 = (f32[512]{0:T(512)S(1)}, f32[512]{0:T(512)}, u32[]{:S(2)}) copy-start(f32[512]{0:T(512)} %param.17) | copy-start | bytes 6148
  6.5 122.3 %all-gather.3.cloned.1.call-start = ((), (), s32[]{:S(2)}) async-start(), calls=%async_computation | async-start | bytes 8912896 | tf_op jit(solution)/shard_map/all_gather | solution.py:59
  7.3 239.0 %all-gather.5.cloned.1.call-start = ((), (), s32[]{:S(2)}) async-start(), calls=%async_computation.1 | async-start | bytes 8912896 | tf_op jit(solution)/shard_map/all_gather | solution.py:64
  17.3 228.9 %copy-start.4 = (f32[512]{0:T(512)S(1)}, f32[512]{0:T(512)}, u32[]{:S(2)}) copy-start(f32[512]{0:T(512)} %param.18) | copy-start | bytes 6148
  254.3 16.2 %copy-start.2 = (bf16[2,256,512]{1,2,0:T(8,128)(2,1)S(1)}, bf16[2,256,512]{1,2,0:T(8,128)(2,1)}, u32[]{:S(2)}) copy-start(bf16[2,256,512]{1,2,0:T(8,128)(2,1)} %copy.25) | copy-start | bytes 1572868
  257.2 3.2 copy-start.1
  270.5 3.8 collective-permute-start
  286.3 10.5 %collective-permute-start = (bf16[2,256,512]{1,2,0:T(8,128)(2,1)S(1)}, bf16[2,256,512]{1,2,0:T(8,128)(2,1)S(1)}, u32[]{:S(2)}, u32[]{:S(2)}) collective-permute-start(bf16[2,256,512]{1,2,0:T(8,128)(2,1)S(1)} %get-tuple-element.419), channel_id=1, source_target_pairs={{0,1},{1,2},{2,3},{3,4},{4,5},{5,6},{6,7},{7,8},{8,9},{9,10},{10,1... | collective-permute-start | bytes 1572872 | tf_op jit(solution)/shard_map/while/body/eval_jaxpr/ppermute | solution.py:19
  308.6 10.5 %collective-permute-start = (bf16[2,256,512]{1,2,0:T(8,128)(2,1)S(1)}, bf16[2,256,512]{1,2,0:T(8,128)(2,1)S(1)}, u32[]{:S(2)}, u32[]{:S(2)}) collective-permute-start(bf16[2,256,512]{1,2,0:T(8,128)(2,1)S(1)} %get-tuple-element.419), channel_id=1, source_target_pairs={{0,1},{1,2},{2,3},{3,4},{4,5},{5,6},{6,7},{7,8},{8,9},{9,10},{10,1... | collective-permute-start | bytes 1572872 | tf_op jit(solution)/shard_map/while/body/eval_jaxpr/ppermute | solution.py:19
  331.1 10.5 %collective-permute-start = (bf16[2,256,512]{1,2,0:T(8,128)(2,1)S(1)}, bf16[2,256,512]{1,2,0:T(8,128)(2,1)S(1)}, u32[]{:S(2)}, u32[]{:S(2)}) collective-permute-start(bf16[2,256,512]{1,2,0:T(8,128)(2,1)S(1)} %get-tuple-element.419), channel_id=1, source_target_pairs={{0,1},{1,2},{2,3},{3,4},{4,5},{5,6},{6,7},{7,8},{8,9},{9,10},{10,1... | collective-permute-start | bytes 1572872 | tf_op jit(solution)/shard_map/while/body/eval_jaxpr/ppermute | solution.py:19
  353.4 10.5 %collective-permute-start = (bf16[2,256,512]{1,2,0:T(8,128)(2,1)S(1)}, bf16[2,256,512]{1,2,0:T(8,128)(2,1)S(1)}, u32[]{:S(2)}, u32[]{:S(2)}) collective-permute-start(bf16[2,256,512]{1,2,0:T(8,128)(2,1)S(1)} %get-tuple-element.419), channel_id=1, source_target_pairs={{0,1},{1,2},{2,3},{3,4},{4,5},{5,6},{6,7},{7,8},{8,9},{9,10},{10,1... | collective-permute-start | bytes 1572872 | tf_op jit(solution)/shard_map/while/body/eval_jaxpr/ppermute | solution.py:19
  375.9 3.8 collective-permute-start
  379.7 5.4 collective-permute-start
  385.1 10.5 %collective-permute-start = (bf16[2,256,512]{1,2,0:T(8,128)(2,1)S(1)}, bf16[2,256,512]{1,2,0:T(8,128)(2,1)S(1)}, u32[]{:S(2)}, u32[]{:S(2)}) collective-permute-start(bf16[2,256,512]{1,2,0:T(8,128)(2,1)S(1)} %get-tuple-element.419), channel_id=1, source_target_pairs={{0,1},{1,2},{2,3},{3,4},{4,5},{5,6},{6,7},{7,8},{8,9},{9,10},{10,1... | collective-permute-start | bytes 1572872 | tf_op jit(solution)/shard_map/while/body/eval_jaxpr/ppermute | solution.py:19
  395.7 10.5 %collective-permute-start = (bf16[2,256,512]{1,2,0:T(8,128)(2,1)S(1)}, bf16[2,256,512]{1,2,0:T(8,128)(2,1)S(1)}, u32[]{:S(2)}, u32[]{:S(2)}) collective-permute-start(bf16[2,256,512]{1,2,0:T(8,128)(2,1)S(1)} %get-tuple-element.419), channel_id=1, source_target_pairs={{0,1},{1,2},{2,3},{3,4},{4,5},{5,6},{6,7},{7,8},{8,9},{9,10},{10,1... | collective-permute-start | bytes 1572872 | tf_op jit(solution)/shard_map/while/body/eval_jaxpr/ppermute | solution.py:19
  406.2 10.5 %collective-permute-start = (bf16[2,256,512]{1,2,0:T(8,128)(2,1)S(1)}, bf16[2,256,512]{1,2,0:T(8,128)(2,1)S(1)}, u32[]{:S(2)}, u32[]{:S(2)}) collective-permute-start(bf16[2,256,512]{1,2,0:T(8,128)(2,1)S(1)} %get-tuple-element.419), channel_id=1, source_target_pairs={{0,1},{1,2},{2,3},{3,4},{4,5},{5,6},{6,7},{7,8},{8,9},{9,10},{10,1... | collective-permute-start | bytes 1572872 | tf_op jit(solution)/shard_map/while/body/eval_jaxpr/ppermute | solution.py:19
  416.8 10.5 %collective-permute-start = (bf16[2,256,512]{1,2,0:T(8,128)(2,1)S(1)}, bf16[2,256,512]{1,2,0:T(8,128)(2,1)S(1)}, u32[]{:S(2)}, u32[]{:S(2)}) collective-permute-start(bf16[2,256,512]{1,2,0:T(8,128)(2,1)S(1)} %get-tuple-element.419), channel_id=1, source_target_pairs={{0,1},{1,2},{2,3},{3,4},{4,5},{5,6},{6,7},{7,8},{8,9},{9,10},{10,1... | collective-permute-start | bytes 1572872 | tf_op jit(solution)/shard_map/while/body/eval_jaxpr/ppermute | solution.py:19
  427.3 79.8 %collective-permute-start = (bf16[2,256,512]{1,2,0:T(8,128)(2,1)S(1)}, bf16[2,256,512]{1,2,0:T(8,128)(2,1)S(1)}, u32[]{:S(2)}, u32[]{:S(2)}) collective-permute-start(bf16[2,256,512]{1,2,0:T(8,128)(2,1)S(1)} %get-tuple-element.419), channel_id=1, source_target_pairs={{0,1},{1,2},{2,3},{3,4},{4,5},{5,6},{6,7},{7,8},{8,9},{9,10},{10,1... | collective-permute-start | bytes 1572872 | tf_op jit(solution)/shard_map/while/body/eval_jaxpr/ppermute | solution.py:19
  519.1 12.6 %collective-permute-start = (bf16[2,256,512]{1,2,0:T(8,128)(2,1)S(1)}, bf16[2,256,512]{1,2,0:T(8,128)(2,1)S(1)}, u32[]{:S(2)}, u32[]{:S(2)}) collective-permute-start(bf16[2,256,512]{1,2,0:T(8,128)(2,1)S(1)} %get-tuple-element.419), channel_id=1, source_target_pairs={{0,1},{1,2},{2,3},{3,4},{4,5},{5,6},{6,7},{7,8},{8,9},{9,10},{10,1... | collective-permute-start | bytes 1572872 | tf_op jit(solution)/shard_map/while/body/eval_jaxpr/ppermute | solution.py:19
  543.6 12.6 %collective-permute-start = (bf16[2,256,512]{1,2,0:T(8,128)(2,1)S(1)}, bf16[2,256,512]{1,2,0:T(8,128)(2,1)S(1)}, u32[]{:S(2)}, u32[]{:S(2)}) collective-permute-start(bf16[2,256,512]{1,2,0:T(8,128)(2,1)S(1)} %get-tuple-element.419), channel_id=1, source_target_pairs={{0,1},{1,2},{2,3},{3,4},{4,5},{5,6},{6,7},{7,8},{8,9},{9,10},{10,1... | collective-permute-start | bytes 1572872 | tf_op jit(solution)/shard_map/while/body/eval_jaxpr/ppermute | solution.py:19
  568.1 12.6 %collective-permute-start = (bf16[2,256,512]{1,2,0:T(8,128)(2,1)S(1)}, bf16[2,256,512]{1,2,0:T(8,128)(2,1)S(1)}, u32[]{:S(2)}, u32[]{:S(2)}) collective-permute-start(bf16[2,256,512]{1,2,0:T(8,128)(2,1)S(1)} %get-tuple-element.419), channel_id=1, source_target_pairs={{0,1},{1,2},{2,3},{3,4},{4,5},{5,6},{6,7},{7,8},{8,9},{9,10},{10,1... | collective-permute-start | bytes 1572872 | tf_op jit(solution)/shard_map/while/body/eval_jaxpr/ppermute | solution.py:19
Sparse Core Ops, SparseCore 0:
  9.8 119.0 all-gather.2
  131.3 114.8 all-gather.4
where the time goes:
time: 613 us; the launch traced here: 609 us
  waiting for transfers between devices  394 us (64%)
  matrix products  94.2 us (15%)
  other arithmetic  52.1 us (8%)
  local copies, waits for them, and re-layouts  24.8 us (4%)
  starting transfers between devices  19.4 us (3%)
  between operations  14.2 us (2%)
  loops' own time  10.8 us (2%)
    ppermute x15, waiting for transfers between devices, passed_along(): return lax.ppermute(x, axis, pairs)  172 us
    all_gather x1, waiting for transfers between devices, body(): lax.all_gather(key_projection_weight, 'dp', axis=0, tiled=True)  112 us
    all_gather x1, waiting for transfers between devices, body(): lax.all_gather(value_projection_weight, 'dp', axis=0, tiled=True)  109 us
    dot_general x10, matrix products, update(): jnp.einsum('tkgs,skd->tkgd', expd.astype(jnp.bfloat16), value_portion, pr...  63.9 us
    ppermute x15, starting transfers between devices, passed_along(): return lax.ppermute(x, axis, pairs)  19.4 us
    reduce_sum x10, other arithmetic, update(): row_total = row_total * factor + jnp.sum(expd, axis=-1)  18.6 us
    dot_general x10, matrix products, update(): jnp.einsum('tkgd,skd->tkgs', query_head_values, key_portion, preferred_el...  16.3 us
  transfers between devices with their start and end apart: 17, of which 17 were waited for; matrix products, arithmetic and copies ran while one was open for 5% of the time, Pallas kernels for 0%

commit v1 on v0

v1 whole, which is shorter than its diff:
```python
import functools
import math

import jax
import jax.numpy as jnp
from jax import lax
from jax.experimental import pallas as pl
from jax.experimental.pallas import tpu as pltpu
from jax.sharding import PartitionSpec as P

MESH = pl.DeviceIdType.MESH
D = 128
BLK = 128
ROPE_BASE = 1000000.0
BIG = 1e30
SCALE = math.log2(math.e) / math.sqrt(D)
VMEM_LIMIT = 56 * 1024 * 1024


def rope_tables(first, count):
    half = D // 2
    frequency = ROPE_BASE ** (-(jnp.arange(half, dtype=jnp.float32) * 2.0 / D))
    positions = (first + jnp.arange(count, dtype=jnp.int32)).astype(jnp.float32)
    angles = positions[:, None] * frequency[None, :]
    cos, sin = jnp.cos(angles), jnp.sin(angles)
    return jnp.concatenate([cos, cos], axis=1), jnp.concatenate([-sin, sin], axis=1)


def gather_kernel(
    hid, q, wk, wv, bk, bv, cos, sin, kv_out, q2,
    hbuf, wbuf, acc, kv,
    lsem, hsend, hrecv, wsend, wrecv, ksend, krecv,
):
    dp, ctx = lax.axis_index("dp"), lax.axis_index("ctx")
    x, zh = dp // 4, dp % 4
    zl, y, core = ctx // 8, (ctx // 2) % 4, ctx % 2
    z = 2 * zh + zl
    m = zl * 4 + y

    def zdev(at):
        return (x * 4 + at // 2, (at % 2) * 8 + ctx % 8)

    xp, xm = (((x + 1) % 4) * 4 + zh, ctx), (((x + 3) % 4) * 4 + zh, ctx)
    zp, zm = zdev((z + 1) % 8), zdev((z + 7) % 8)
    yp = (dp, zl * 8 + ((y + 1) % 4) * 2 + core)
    ym = (dp, zl * 8 + ((y + 3) % 4) * 2 + core)
    sib = (dp, ctx + 1 - 2 * core)
    near = (xp, xm, zp, zm, yp, ym, sib)

    def weights_in(g, which):
        head = pl.multiple_of((2 * core + g) * D, D)
        src = (wk, wv)[which].at[:, pl.ds(head, D)]
        return pltpu.make_async_copy(src, wbuf.at[g, dp, :, pl.ds(which * D, D)], lsem.at[2 * g + which])

    def hidden_in(j):
        at = (x + j) % 4
        cols = pl.ds(pl.multiple_of(at * 2048, 2048), 2048)
        rows = pl.ds(pl.multiple_of(core * 256, 256), 256)
        local = pltpu.make_async_copy(hid.at[:, cols], hbuf.at[at, rows], lsem.at[4 + j])
        remote = pltpu.make_async_remote_copy(
            hid.at[:, cols], hbuf.at[at, rows], hsend.at[j], hrecv.at[j], device_id=sib, device_id_type=MESH)
        return local, remote

    def hidden_landed(j):
        at = (x + j) % 4
        cols = pl.ds(pl.multiple_of(at * 2048, 2048), 2048)
        rows = pl.ds(pl.multiple_of((1 - core) * 256, 256), 256)
        return pltpu.make_async_remote_copy(
            hid.at[:, cols], hbuf.at[at, rows], hsend.at[j], hrecv.at[j], device_id=sib, device_id_type=MESH)

    my_rows = pl.ds(pl.multiple_of(core * 256, 256), 256)
    q_local = pltpu.make_async_copy(
        q.at[:, pl.ds(pl.multiple_of(core * 2048, 2048), 2048)], q2.at[my_rows], lsem.at[8])
    q_remote = pltpu.make_async_remote_copy(
        q.at[:, pl.ds(pl.multiple_of((1 - core) * 2048, 2048), 2048)], q2.at[my_rows],
        hsend.at[4], hrecv.at[4], device_id=sib, device_id_type=MESH)

    for g in range(2):
        for which in range(2):
            weights_in(g, which).start()

    barrier = pltpu.get_barrier_semaphore()
    for to in near:
        pl.semaphore_signal(barrier, inc=1, device_id=to, device_id_type=MESH)
    pl.semaphore_wait(barrier, len(near))

    def lane(k):
        j = k - 1
        return j + j // 2 - 2 * (j // 3)

    def row_of(base, kind):
        return base + (128 if kind == 3 else 0), (256 if kind < 2 else 128)

    def piece(g, shard, base, kind):
        start, size = row_of(base, kind)
        return wbuf.at[g, shard, pl.ds(start, size)]

    def copy(ref, to, g, task, kind):
        at = (g * 10 + task) * 4 + kind
        return pltpu.make_async_remote_copy(
            ref, ref, wsend.at[at], wrecv.at[at], device_id=to, device_id_type=MESH)

    def x_at(k):
        return (zh, 0) if isinstance(k, int) and k == 0 else ((zh + lane(k)) % 4, 256)

    def z_at(k):
        return (x, 256) if isinstance(k, int) and k == 0 else ((x + lane(k)) % 4, 0)

    def x_send(g, k, kind):
        at, base = x_at(k)
        shard = ((x + (0, 0, 3, 1)[kind]) % 4) * 4 + at
        copy(piece(g, shard, base, kind), (xp, xm)[kind % 2], g, k, kind).start()

    def x_wait(g, k, kind):
        at, base = x_at(k)
        shard = ((x + (3, 1, 2, 2)[kind]) % 4) * 4 + at
        copy(piece(g, shard, base, kind), xp, g, k, kind).wait_recv()

    def z_send(g, k, kind):
        at, base = z_at(k)
        off = (zl + 3, zl, zl + 2, zl + 1)[kind]
        shard = at * 4 + (zh + off) % 4
        copy(piece(g, shard, base, kind), (zp, zm)[kind % 2], g, k + 5, kind).start()

    def z_wait(g, k, kind):
        at, base = z_at(k)
        shard = at * 4 + (zh + (3, 1, 2, 2)[kind]) % 4
        copy(piece(g, shard, base, kind), zp, g, k + 5, kind).wait_recv()

    def x_start(g, k):
        x_send(g, k, 0)
        x_send(g, k, 1)

    def z_start(g, k):
        @pl.when(zl == 1)
        def _():
            z_send(g, k, 0)

        @pl.when(zl == 0)
        def _():
            z_send(g, k, 1)

    def z_step(g, k, kind):
        z_wait(g, k, kind)
        even, odd = ((0, 2), (3, 1), (2, None), (None, 3))[kind]
        if even is not None:
            @pl.when(zl == 0)
            def _():
                z_send(g, k, even)
        if odd is not None:
            @pl.when(zl == 1)
            def _():
                z_send(g, k, odd)

    def x_step(g, k, kind):
        x_wait(g, k, kind)
        if kind < 2:
            x_send(g, k, kind + 2)

    def begin(g):
        weights_in(g, 0).wait()
        weights_in(g, 1).wait()
        x_start(g, 0)
        z_start(g, 0)
        x_start(g, 1)
        z_start(g, 1)

    def first(g):
        x_step(g, 0, 0)
        z_start(g, 3)
        z_step(g, 0, 0)
        x_start(g, 3)
        x_step(g, 0, 1)
        z_start(g, 2)
        z_step(g, 0, 1)
        x_start(g, 2)
        x_step(g, 0, 2)
        x_step(g, 0, 3)
        z_start(g, 4)
        z_step(g, 0, 2)
        z_step(g, 0, 3)
        x_start(g, 4)

    def later(g, k):
        for kind in range(4):
            x_step(g, k, kind)
            z_step(g, k, kind)

    def product(g, sx, sz, base):
        return jnp.dot(
            hbuf[sx, :, pl.ds(pl.multiple_of(sz * 512 + base, 256), 256)],
            wbuf[g, sx * 4 + sz, pl.ds(base, 256)],
            preferred_element_type=jnp.float32,
        )

    def multiply(g, k):
        at, base = x_at(k)
        total = acc[...]
        for off in (3, 1, 2):
            total += product(g, (x + off) % 4, at, base)
        at, base = z_at(k)
        for off in (3, 1, 2):
            total += product(g, at, (zh + off) % 4, base)
        acc[...] = total

    def own(g):
        acc[...] = product(g, x, zh, 0) + product(g, x, zh, 256)

    def kcopy(g, at, kind, unit, to):
        start, size = (256 if kind == 3 else 0), (512 if kind < 2 else 256)
        ref = kv.at[g, unit, pl.ds(start, size)]
        n = g * 9 + at + kind
        return pltpu.make_async_remote_copy(ref, ref, ksend.at[n], krecv.at[n], device_id=to, device_id_type=MESH)

    def k_send(g, line, kind):
        unit = line * 4 + (y + (0, 0, 3, 1)[kind]) % 4
        at = 4 if isinstance(line, int) else 0
        kcopy(g, at, kind, unit, (yp, ym)[kind % 2]).start()

    def k_wait(g, line, kind):
        unit = line * 4 + (y + (3, 1, 2, 2)[kind]) % 4
        at = 4 if isinstance(line, int) else 0
        kcopy(g, at, kind, unit, yp).wait_recv()

    def cross(g, unit):
        ref = kv.at[g, unit]
        n = g * 9 + 8
        to = (dp, ctx % 8 + 8)
        return pltpu.make_async_remote_copy(ref, ref, ksend.at[n], krecv.at[n], device_id=to, device_id_type=MESH)

    def kv_begin(g):
        total = acc[...]
        head = 2 * core + g
        key = total[:, :D] + bk[head]
        turned = jnp.concatenate([key[:, D // 2:], key[:, : D // 2]], axis=1)
        key = key * cos[...] + turned * sin[...]
        value = total[:, D:] + bv[head]
        kv[g, m] = jnp.concatenate([key, value], axis=1).astype(jnp.bfloat16)

        @pl.when(zl == 0)
        def _():
            cross(g, m).start()
        k_send(g, zl, 0)
        k_send(g, zl, 1)

    def kv_one(g):
        for kind in range(2):
            k_wait(g, zl, kind)
            k_send(g, zl, kind + 2)

        @pl.when(zl == 1)
        def _():
            cross(g, y).wait_recv()
            k_send(g, 0, 0)
            k_send(g, 0, 1)

    def kv_two(g):
        k_wait(g, zl, 2)
        k_wait(g, zl, 3)

        @pl.when(zl == 1)
        def _():
            for kind in range(2):
                k_wait(g, 0, kind)
                k_send(g, 0, kind + 2)

    def kv_three(g):
        @pl.when(zl == 1)
        def _():
            k_wait(g, 0, 2)
            k_wait(g, 0, 3)

    def kv_leave(g):
        return pltpu.make_async_copy(kv.at[g], kv_out.at[g], lsem.at[9 + g])

    def kv_sent(g):
        for kind in range(4):
            kcopy(g, 0, kind, m, yp).wait_send()

        @pl.when(zl == 1)
        def _():
            for kind in range(4):
                kcopy(g, 4, kind, m, yp).wait_send()

        @pl.when(zl == 0)
        def _():
            cross(g, m).wait_send()

    begin(0)
    for j in (0, 1, 3, 2):
        local, remote = hidden_in(j)
        local.start()
        remote.start()
    q_local.start()
    q_remote.start()
    first(0)
    later(0, 1)
    for j in (0, 1, 3, 2):
        hidden_in(j)[0].wait()
        hidden_landed(j).wait_recv()
    own(0)
    multiply(0, 0)
    multiply(0, 1)

    def step0(k, carry):
        later(0, k)
        multiply(0, k)
        return carry

    lax.fori_loop(2, 4, step0, 0)
    begin(1)
    later(0, 4)
    multiply(0, 4)
    kv_begin(0)
    first(1)
    own(1)
    multiply(1, 0)
    kv_one(0)
    later(1, 1)
    multiply(1, 1)
    kv_two(0)
    later(1, 2)
    multiply(1, 2)
    kv_three(0)

    kv_leave(0).start()

    def step1(k, carry):
        later(1, k)
        multiply(1, k)
        return carry

    lax.fori_loop(3, 5, step1, 0)
    kv_begin(1)
    kv_one(1)
    kv_two(1)
    kv_three(1)
    kv_leave(1).start()

    def drain(task, carry):
        for kind in range(4):
            start, size = row_of(0, kind)
            ref = wbuf.at[0, 0, pl.ds(start, size)]
            at = task * 4 + kind
            pltpu.make_async_remote_copy(
                ref, ref, wsend.at[at], wrecv.at[at], device_id=xp, device_id_type=MESH).wait_send()
        return carry

    lax.fori_loop(0, 20, drain, 0)
    for g in range(2):
        kv_sent(g)
    for j in range(4):
        hidden_in(j)[1].wait_send()
    q_local.wait()
    q_remote.wait_send()
    other = pl.ds(pl.multiple_of((1 - core) * 256, 256), 256)
    pltpu.make_async_remote_copy(
        q.at[:, pl.ds(0, 2048)], q2.at[other], hsend.at[4], hrecv.at[4], device_id=sib, device_id_type=MESH).wait_recv()
    kv_leave(0).wait()
    kv_leave(1).wait()


def gathered(hid, q, wk, wv, bk, bv, cos, sin):
    vmem, anywhere = pl.BlockSpec(memory_space=pltpu.VMEM), pl.BlockSpec(memory_space=pl.ANY)
    bf16 = jnp.bfloat16
    return pl.pallas_call(
        gather_kernel,
        out_shape=(jax.ShapeDtypeStruct((2, 8, 512, 256), bf16), jax.ShapeDtypeStruct((512, 2048), bf16)),
        in_specs=[anywhere] * 4 + [vmem] * 4,
        out_specs=(anywhere, anywhere),
        scratch_shapes=[
            pltpu.VMEM((4, 512, 2048), bf16),
            pltpu.VMEM((2, 16, 512, 256), bf16),
            pltpu.VMEM((512, 256), jnp.float32),
            pltpu.VMEM((2, 8, 512, 256), bf16),
            pltpu.SemaphoreType.DMA((11,)),
            pltpu.SemaphoreType.DMA((5,)),
            pltpu.SemaphoreType.DMA((5,)),
            pltpu.SemaphoreType.DMA((80,)),
            pltpu.SemaphoreType.DMA((80,)),
            pltpu.SemaphoreType.DMA((18,)),
            pltpu.SemaphoreType.DMA((18,)),
        ],
        compiler_params=pltpu.CompilerParams(
            collective_id=0, has_side_effects=True, vmem_limit_bytes=VMEM_LIMIT),
        name="gather",
    )(hid, q, wk, wv, bk, bv, cos, sin)


def attend_kernel(segs, place, q, kv, out, scores, peak, total, acc):
    b = pl.program_id(1)
    t = place[0] + b
    mine = segs[t]

    def count(i, carry):
        before = (i < t).astype(jnp.int32)
        premise = (segs[i] == 0).astype(jnp.int32)
        same = (segs[i] == mine).astype(jnp.int32)
        return (carry[0] + before * premise, carry[1] + before * (1 - premise) * same)

    p, o = lax.fori_loop(0, 32, count, (jnp.int32(0), jnp.int32(0)))
    n = p + o
    full = n // 2

    def slot(j):
        return pl.multiple_of(jnp.where(j < p, j, j - p + t - o) * BLK, BLK)

    peak[...] = jnp.full_like(peak, -BIG)

    def score(c, first, second, mask):
        keys = jnp.concatenate([kv[0, pl.ds(first, BLK), :D], kv[0, pl.ds(second, BLK), :D]], axis=0)
        for j in range(8):
            rows = pl.ds(j * BLK, BLK)
            s = lax.dot_general(
                q[:, j * D:(j + 1) * D], keys, (((1,), (1,)), ((), ())), preferred_element_type=jnp.float32) * SCALE
            if mask is not None:
                s = jnp.where(mask, s, -BIG)
            scores[c, rows] = s
            peak[rows] = jnp.maximum(peak[rows], jnp.maximum(s[:, :BLK], s[:, BLK:]))

    def one(c, carry):
        score(c, slot(2 * c), slot(2 * c + 1), None)
        return carry

    lax.fori_loop(0, full, one, 0)
    odd = n % 2
    extra, diagonal = slot(jnp.maximum(n - 1, 0)), pl.multiple_of(t * BLK, BLK)
    row = lax.broadcasted_iota(jnp.int32, (BLK, 2 * BLK), 0)
    col = lax.broadcasted_iota(jnp.int32, (BLK, 2 * BLK), 1)
    least = jnp.where(col < BLK, jnp.where(odd == 1, -1, BLK), col - BLK)
    score(full, extra, diagonal, row >= least)

    peak[...] = jnp.broadcast_to(jnp.max(peak[...], axis=1, keepdims=True), peak.shape)
    total[...] = jnp.zeros_like(total)
    acc[...] = jnp.zeros_like(acc)

    def weigh(c, first, second):
        values = jnp.concatenate([kv[0, pl.ds(first, BLK), D:], kv[0, pl.ds(second, BLK), D:]], axis=0)
        for j in range(8):
            rows = pl.ds(j * BLK, BLK)
            top = peak[rows]
            left = jnp.exp2(scores[c, rows, :BLK] - top)
            right = jnp.exp2(scores[c, rows, BLK:] - top)
            total[rows] += left + right
            weights = jnp.concatenate([left, right], axis=1).astype(jnp.bfloat16)
            acc[rows] += jnp.dot(weights, values, preferred_element_type=jnp.float32)

    def two(c, carry):
        weigh(c, slot(2 * c), slot(2 * c + 1))
        return carry

    lax.fori_loop(0, full, two, 0)
    weigh(full, extra, diagonal)
    for j in range(8):
        rows = pl.ds(j * BLK, BLK)
        out[:, j * D:(j + 1) * D] = (acc[rows] / jnp.sum(total[rows], axis=1, keepdims=True)).astype(jnp.bfloat16)


def attended(segs, place, q2, kv):
    return pl.pallas_call(
        attend_kernel,
        out_shape=jax.ShapeDtypeStruct((512, 2048), jnp.bfloat16),
        grid_spec=pltpu.PrefetchScalarGridSpec(
            num_scalar_prefetch=2,
            grid=(2, 4),
            in_specs=[
                pl.BlockSpec((BLK, 8 * D), lambda g, b, *_: (b, g)),
                pl.BlockSpec((1, 4096, 2 * D), lambda g, b, *_: (g, 0, 0)),
            ],
            out_specs=pl.BlockSpec((BLK, 8 * D), lambda g, b, *_: (b, g)),
            scratch_shapes=[
                pltpu.VMEM((13, 8 * BLK, 2 * BLK), jnp.float32),
                pltpu.VMEM((8 * BLK, BLK), jnp.float32),
                pltpu.VMEM((8 * BLK, BLK), jnp.float32),
                pltpu.VMEM((8 * BLK, D), jnp.float32),
            ],
        ),
        compiler_params=pltpu.CompilerParams(vmem_limit_bytes=VMEM_LIMIT),
        name="attend",
    )(segs, place, q2, kv)


def swap_kernel(mine, out, lsem, ssem, rsem):
    dp, ctx = lax.axis_index("dp"), lax.axis_index("ctx")
    core = ctx % 2
    sib = (dp, ctx + 1 - 2 * core)
    barrier = pltpu.get_barrier_semaphore()
    pl.semaphore_signal(barrier, inc=1, device_id=sib, device_id_type=MESH)
    pl.semaphore_wait(barrier, 1)
    cols = pl.ds(pl.multiple_of(core * 2048, 2048), 2048)
    others = pl.ds(pl.multiple_of((1 - core) * 2048, 2048), 2048)
    local = pltpu.make_async_copy(mine.at[pl.ds(pl.multiple_of(core * 256, 256), 256)], out.at[:, cols], lsem)
    src = mine.at[pl.ds(pl.multiple_of((1 - core) * 256, 256), 256)]
    remote = pltpu.make_async_remote_copy(src, out.at[:, cols], ssem, rsem, device_id=sib, device_id_type=MESH)
    landed = pltpu.make_async_remote_copy(src, out.at[:, others], ssem, rsem, device_id=sib, device_id_type=MESH)
    remote.start()
    local.start()
    local.wait()
    remote.wait_send()
    landed.wait_recv()


def swapped(mine):
    anywhere = pl.BlockSpec(memory_space=pl.ANY)
    return pl.pallas_call(
        swap_kernel,
        out_shape=jax.ShapeDtypeStruct((256, 4096), jnp.bfloat16),
        in_specs=[anywhere],
        out_specs=anywhere,
        scratch_shapes=[pltpu.SemaphoreType.DMA, pltpu.SemaphoreType.DMA, pltpu.SemaphoreType.DMA],
        compiler_params=pltpu.CompilerParams(collective_id=1, has_side_effects=True),
        name="swap",
    )(mine)


def body(hidden_in, queries, wk, wv, bk, bv, segs):
    ctx = lax.axis_index("ctx")
    cos, sin = rope_tables((ctx // 2) * 512, 512)
    kv, q2 = gathered(hidden_in[0], queries[0], wk, wv, bk.reshape(4, 1, D), bv.reshape(4, 1, D), cos, sin)
    place = jnp.reshape((ctx // 2) * 4, (1,)).astype(jnp.int32)
    mine = attended(segs[0], place, q2, kv.reshape(2, 4096, 256))
    return swapped(mine)[None]


def solution(mesh):
    placed = (P("dp", "ctx", None), P("dp", "ctx", None), P("dp", None), P("dp", None), P(), P(), P("dp", None))
    return jax.shard_map(body, mesh=mesh, in_specs=placed, out_specs=P("dp", "ctx", None), check_vma=False)
```

time: 613 us -> 296 us (0.48)
  the two profiles are of different devices: /device:TPU:61 before, /device:TPU:56 now
where the time goes in v1:
time: 296 us; the launch traced here: 295 us
  Pallas kernels  290 us (98%)
  local copies, waits for them, and re-layouts  3.13 us (1%)
    pallas_call x1, Pallas kernels, gathered(): pl.pallas_call(gather_kernel, out_shape=(jax.ShapeDtypeStruct((2, 8, 512,...  201 us
    pallas_call x1, Pallas kernels, attended(): pl.pallas_call(attend_kernel, out_shape=jax.ShapeDtypeStruct((512, 2048),...  56 us
    pallas_call x1, Pallas kernels, swapped(): pl.pallas_call(swap_kernel, out_shape=jax.ShapeDtypeStruct((256, 4096), j...  32.9 us

profile of v1, /device:TPU:56, one launch (start us, length us, event | category | flops | bytes accessed | tf_op | source)
XLA Modules:
  0.0 294.8 jit_solution(7422076082734576778)
XLA Ops:
  0.0 1.0 fusion
  1.0 1.0 pad_maximum_fusion
  2.0 200.8 %gather.1 = (bf16[2,8,512,256]{3,2,1,0:T(8,128)(2,1)}, bf16[512,2048]{1,0:T(8,128)(2,1)}) custom-call(bf16[256,8192]{1,0:T(8,128)(2,1)} %bitcast.9, bf16[256,4096]{1,0:T(8,128)(2,1)} %bitcast.11, bf16[512,512]{1,0:T(8,128)(2,1)} %wk.1, bf16[512,512]{1,0:T(8,128)(2,1)} %wv.1, f32[4,1,128]{2,1,0:T(1,128)} %bitcast.12, f32[4,1,128]{2,1,0:T(1,128)} %bitcast.13, ...), custom_call_target="tpu_custom_call" | custom-call | tf_op jit(solution)/shard_map/gather/pallas_call | solution.py:366
  202.8 56.0 %attend.1.mine = bf16[512,2048]{1,0:T(8,128)(2,1)} custom-call(s32[32]{0:T(128)} %bitcast.14, s32[1]{0:T(128)} %bitcast.1.place, bf16[512,2048]{1,0:T(8,128)(2,1)} %get-tuple-element.7.q, bf16[2,4096,256]{2,1,0:T(8,128)(2,1)} %bitcast.10), custom_call_target="tpu_custom_call" | custom-call | tf_op jit(solution)/shard_map/attend/pallas_call | solution.py:460
  258.8 32.9 %swap.1 = bf16[256,4096]{1,0:T(8,128)(2,1)} custom-call(bf16[512,2048]{1,0:T(8,128)(2,1)} %attend.1.mine), custom_call_target="tpu_custom_call" | custom-call | tf_op jit(solution)/shard_map/swap/pallas_call | solution.py:505
  291.7 3.1 %copy.9 = bf16[1,256,4096]{2,1,0:T(8,128)(2,1)} copy(bf16[1,256,4096]{2,1,0:T(8,128)(2,1)} %bitcast.8) | data formatting | bytes 4194304
  (2 shorter events, 0.0 us)

commit v2 on v1

v2 whole, which is shorter than its diff:
```python
import functools
import math

import jax
import jax.numpy as jnp
from jax import lax
from jax.experimental import pallas as pl
from jax.experimental.pallas import tpu as pltpu
from jax.sharding import PartitionSpec as P

MESH = pl.DeviceIdType.MESH
D = 128
BLK = 128
NBLK = 32
MOST = 12
ROPE_BASE = 1000000.0
BIG = 1e30
SCALE = math.log2(math.e) / math.sqrt(D)
VMEM_LIMIT = 56 * 1024 * 1024


def rope_tables(first, count):
    half = D // 2
    frequency = ROPE_BASE ** (-(jnp.arange(half, dtype=jnp.float32) * 2.0 / D))
    positions = (first + jnp.arange(count, dtype=jnp.int32)).astype(jnp.float32)
    angles = positions[:, None] * frequency[None, :]
    cos, sin = jnp.cos(angles), jnp.sin(angles)
    return jnp.concatenate([cos, cos], axis=1), jnp.concatenate([-sin, sin], axis=1)


def whole_kernel(
    slots, biases, hid, q, wk, wv, bk, bv, cos, sin, out,
    hbuf, wbuf, acc, kv0, kv1, q2, scores, peak, total, weighted, tiles,
    lsem, hsend, hrecv, wsend, wrecv, ksend, krecv, osend, orecv,
):
    kv = (kv0, kv1)
    dp, ctx = lax.axis_index("dp"), lax.axis_index("ctx")
    x, zh = dp // 4, dp % 4
    zl, y, core = ctx // 8, (ctx // 2) % 4, ctx % 2
    z = 2 * zh + zl
    m = zl * 4 + y

    def zdev(at):
        return (x * 4 + at // 2, (at % 2) * 8 + ctx % 8)

    xp, xm = (((x + 1) % 4) * 4 + zh, ctx), (((x + 3) % 4) * 4 + zh, ctx)
    zp, zm = zdev((z + 1) % 8), zdev((z + 7) % 8)
    yp = (dp, zl * 8 + ((y + 1) % 4) * 2 + core)
    ym = (dp, zl * 8 + ((y + 3) % 4) * 2 + core)
    sib = (dp, ctx + 1 - 2 * core)
    neighbours = (xp, xm, zp, zm, yp, ym, sib)

    def weights_in(g, which):
        head = pl.multiple_of((2 * core + g) * D, D)
        src = (wk, wv)[which].at[:, pl.ds(head, D)]
        return pltpu.make_async_copy(src, wbuf.at[g, dp, :, pl.ds(which * D, D)], lsem.at[2 * g + which])

    def hidden_in(j):
        at = (x + j) % 4
        cols = pl.ds(pl.multiple_of(at * 2048, 2048), 2048)
        rows = pl.ds(pl.multiple_of(core * 256, 256), 256)
        local = pltpu.make_async_copy(hid.at[:, cols], hbuf.at[at, rows], lsem.at[4 + j])
        remote = pltpu.make_async_remote_copy(
            hid.at[:, cols], hbuf.at[at, rows], hsend.at[j], hrecv.at[j], device_id=sib, device_id_type=MESH)
        return local, remote

    def hidden_landed(j):
        at = (x + j) % 4
        cols = pl.ds(pl.multiple_of(at * 2048, 2048), 2048)
        rows = pl.ds(pl.multiple_of((1 - core) * 256, 256), 256)
        return pltpu.make_async_remote_copy(
            hid.at[:, cols], hbuf.at[at, rows], hsend.at[j], hrecv.at[j], device_id=sib, device_id_type=MESH)

    my_rows = pl.ds(pl.multiple_of(core * 256, 256), 256)
    q_local = pltpu.make_async_copy(
        q.at[:, pl.ds(pl.multiple_of(core * 2048, 2048), 2048)], q2.at[my_rows], lsem.at[8])
    q_remote = pltpu.make_async_remote_copy(
        q.at[:, pl.ds(pl.multiple_of((1 - core) * 2048, 2048), 2048)], q2.at[my_rows],
        hsend.at[4], hrecv.at[4], device_id=sib, device_id_type=MESH)

    for g in range(2):
        for which in range(2):
            weights_in(g, which).start()

    barrier = pltpu.get_barrier_semaphore()
    for to in neighbours:
        pl.semaphore_signal(barrier, inc=1, device_id=to, device_id_type=MESH)
    pl.semaphore_wait(barrier, len(neighbours))

    turn = 1 - 2 * zl
    near_z, far_z, across_z = (zh + 4 - turn) % 4, (zh + turn + 4) % 4, (zh + 2) % 4
    before_x, after_x, across_x = (x + 3) % 4, (x + 1) % 4, (x + 2) % 4
    z_places, x_places = (zh, near_z, far_z, across_z), (x, before_x, after_x, across_x)
    near_dev = zdev((z + 8 - turn) % 8)
    far_dev = zdev((z + 8 + turn) % 8)

    def copy(g, shard, start, size, to, task, kind):
        ref = wbuf.at[g, shard, pl.ds(start, size)]
        at = (g * 10 + task) * 4 + kind
        return pltpu.make_async_remote_copy(
            ref, ref, wsend.at[at], wrecv.at[at], device_id=to, device_id_type=MESH)

    def x_base(k):
        return (z_places[max(k - 1, 0)], 0 if k == 0 else 256)

    def z_base(k):
        return (x_places[max(k - 1, 0)], 256 if k == 0 else 0)

    def x_start(g, k):
        at, base = x_base(k)
        for kind, to in ((0, xp), (1, xm)):
            copy(g, x * 4 + at, base, 256, to, k, kind).start()

    def x_level(g, k, level):
        at, base = x_base(k)
        if level == 1:
            for kind, place, to in ((0, before_x, xp), (1, after_x, xm)):
                shard = place * 4 + at
                copy(g, shard, base, 256, to, k, kind).wait_recv()
                copy(g, shard, base + 128 * kind, 128, to, k, kind + 2).start()
        else:
            shard = across_x * 4 + at
            for kind in range(2):
                copy(g, shard, base + 128 * kind, 128, xp, k, kind + 2).wait_recv()

    def z_start(g, k):
        at, base = z_base(k)
        copy(g, at * 4 + zh, base, 256, near_dev, k + 5, 0).start()

    def z_level(g, k, level):
        at, base = z_base(k)
        mine, theirs = base + 128 * zl, base + 128 * (1 - zl)
        if level == 1:
            copy(g, at * 4 + near_z, base, 256, near_dev, k + 5, 0).wait_recv()
            copy(g, at * 4 + near_z, base, 256, far_dev, k + 5, 1).start()
        elif level == 2:
            copy(g, at * 4 + far_z, base, 256, near_dev, k + 5, 1).wait_recv()
            start = pl.multiple_of(theirs, 128)
            copy(g, at * 4 + far_z, start, 128, near_dev, k + 5, 2).start()
        elif level == 3:
            start = pl.multiple_of(mine, 128)
            copy(g, at * 4 + across_z, start, 128, near_dev, k + 5, 2).wait_recv()
            copy(g, at * 4 + across_z, start, 128, far_dev, k + 5, 3).start()
        else:
            start = pl.multiple_of(theirs, 128)
            copy(g, at * 4 + across_z, start, 128, near_dev, k + 5, 3).wait_recv()

    def begin(g):
        weights_in(g, 0).wait()
        weights_in(g, 1).wait()
        for k in range(2):
            z_start(g, k)
            x_start(g, k)

    def step(g, r):
        events = (
            (("x", 0, 1, "z2", "z3"), ("z", 0, 1, "x2"), ("x", 1, 1), ("z", 1, 1)),
            (("x", 0, 2, "z4"), ("z", 0, 2, "x3"), ("z", 1, 2), ("x", 1, 2), ("z", 2, 1), ("z", 3, 1), ("x", 2, 1)),
            (("z", 0, 3), ("z", 1, 3), ("z", 2, 2), ("z", 3, 2), ("z", 4, 1), ("x", 3, 1), ("x", 2, 2)),
            (("z", 0, 4, "x4"), ("z", 1, 4), ("z", 2, 3), ("z", 3, 3), ("z", 4, 2), ("x", 3, 2)),
            (("x", 4, 1), ("z", 4, 3), ("z", 2, 4), ("z", 3, 4)),
            (("x", 4, 2), ("z", 4, 4)),
        )[r - 1]
        for axis, k, level, *then in events:
            (x_level if axis == "x" else z_level)(g, k, level)
            for name in then:
                (x_start if name[0] == "x" else z_start)(g, int(name[1]))

    def product(g, sx, sz, base):
        return jnp.dot(
            hbuf[sx, :, pl.ds(pl.multiple_of(sz * 512 + base, 256), 256)],
            wbuf[g, sx * 4 + sz, pl.ds(base, 256)],
            preferred_element_type=jnp.float32,
        )

    def multiply(g, tasks):
        sums = acc[...]
        for name in tasks:
            k = int(name[1])
            if name[0] == "x":
                at, base = x_base(k)
                for place in x_places[1:]:
                    sums += product(g, place, at, base)
            else:
                at, base = z_base(k)
                for place in z_places[1:]:
                    sums += product(g, at, place, base)
        acc[...] = sums

    def own(g):
        acc[...] = product(g, x, zh, 0) + product(g, x, zh, 256)

    def kcopy(g, at, kind, unit, to):
        start, size = (2 if kind == 3 else 0), (4 if kind < 2 else 2)
        ref = kv[g].at[pl.ds(unit * 4 + start, size)]
        n = g * 9 + at + kind
        return pltpu.make_async_remote_copy(ref, ref, ksend.at[n], krecv.at[n], device_id=to, device_id_type=MESH)

    def k_send(g, line, kind):
        unit = line * 4 + (y + (0, 0, 3, 1)[kind]) % 4
        at = 4 if isinstance(line, int) else 0
        kcopy(g, at, kind, unit, (yp, ym)[kind % 2]).start()

    def k_wait(g, line, kind):
        unit = line * 4 + (y + (3, 1, 2, 2)[kind]) % 4
        at = 4 if isinstance(line, int) else 0
        kcopy(g, at, kind, unit, yp).wait_recv()

    def cross(g, unit):
        ref = kv[g].at[pl.ds(unit * 4, 4)]
        n = g * 9 + 8
        to = (dp, ctx % 8 + 8)
        return pltpu.make_async_remote_copy(ref, ref, ksend.at[n], krecv.at[n], device_id=to, device_id_type=MESH)

    def kv_begin(g):
        sums = acc[...]
        head = 2 * core + g
        key = sums[:, :D] + bk[head]
        turned = jnp.concatenate([key[:, D // 2:], key[:, : D // 2]], axis=1)
        key = key * cos[...] + turned * sin[...]
        value = sums[:, D:] + bv[head]
        kv[g][pl.ds(m * 4, 4)] = jnp.concatenate([key, value], axis=1).astype(jnp.bfloat16).reshape(4, BLK, 2 * D)

        @pl.when(zl == 0)
        def _():
            cross(g, m).start()
        k_send(g, zl, 0)
        k_send(g, zl, 1)

    def kv_one(g):
        for kind in range(2):
            k_wait(g, zl, kind)
            k_send(g, zl, kind + 2)

        @pl.when(zl == 1)
        def _():
            cross(g, y).wait_recv()
            k_send(g, 0, 0)
            k_send(g, 0, 1)

    def kv_two(g):
        k_wait(g, zl, 2)
        k_wait(g, zl, 3)

        @pl.when(zl == 1)
        def _():
            for kind in range(2):
                k_wait(g, 0, kind)
                k_send(g, 0, kind + 2)

    def kv_three(g):
        @pl.when(zl == 1)
        def _():
            k_wait(g, 0, 2)
            k_wait(g, 0, 3)

    def kv_sent(g):
        for kind in range(4):
            kcopy(g, 0, kind, m, yp).wait_send()

        @pl.when(zl == 1)
        def _():
            for kind in range(4):
                kcopy(g, 4, kind, m, yp).wait_send()

        @pl.when(zl == 0)
        def _():
            cross(g, m).wait_send()

    begin(0)
    for j in (0, 1, 3, 2):
        local, remote = hidden_in(j)
        local.start()
        remote.start()
    q_local.start()
    q_remote.start()
    step(0, 1)
    step(0, 2)
    step(0, 3)
    begin(1)
    step(0, 4)
    for j in (0, 1, 3, 2):
        hidden_in(j)[0].wait()
        hidden_landed(j).wait_recv()
    own(0)
    multiply(0, ("x0", "x1", "z0", "z1"))
    step(1, 1)
    step(0, 5)
    multiply(0, ("x2", "x3", "z2", "z3"))
    step(1, 2)
    step(0, 6)
    multiply(0, ("x4", "z4"))
    kv_begin(0)
    step(1, 3)
    own(1)
    multiply(1, ("x0", "x1"))
    kv_one(0)
    step(1, 4)
    multiply(1, ("z0", "z1"))
    kv_two(0)
    step(1, 5)
    multiply(1, ("x2", "x3", "z2", "z3"))
    kv_three(0)
    step(1, 6)
    multiply(1, ("x4", "z4"))
    kv_begin(1)

    q_local.wait()
    others = pl.ds(pl.multiple_of((1 - core) * 256, 256), 256)
    pltpu.make_async_remote_copy(
        q.at[:, pl.ds(0, 2048)], q2.at[others], hsend.at[4], hrecv.at[4], device_id=sib, device_id_type=MESH).wait_recv()

    def attend(g, i):
        b = (i + 2 * (1 - core)) % 4
        t = m * 4 + b
        most = jnp.minimum(t, 2 * MOST - 1) // 2
        q_rows = pl.ds(pl.multiple_of(b * BLK, BLK), BLK)

        peak[...] = jnp.full_like(peak, -BIG)

        def score(c, first, second, less, mask):
            keys = jnp.concatenate([kv[g][first, :, :D], kv[g][second, :, :D]], axis=0)
            for j in range(8):
                rows = pl.ds(j * BLK, BLK)
                s = lax.dot_general(
                    q2[q_rows, g * 1024 + j * D:g * 1024 + (j + 1) * D], keys, (((1,), (1,)), ((), ())),
                    preferred_element_type=jnp.float32) * SCALE
                if mask is not None:
                    s = jnp.where(mask, s, -BIG)
                scores[c, rows] = s
                top = jnp.maximum(s[:, :BLK], s[:, BLK:])
                if mask is None:
                    top = top - less
                peak[rows] = jnp.maximum(peak[rows], top)

        def one(c, carry):
            score(c, slots[b, 2 * c], slots[b, 2 * c + 1], biases[b, c], None)
            return carry

        lax.fori_loop(0, most, one, 0)
        extra, from_row = slots[b, 24], slots[b, 25]
        row = lax.broadcasted_iota(jnp.int32, (BLK, 2 * BLK), 0)
        col = lax.broadcasted_iota(jnp.int32, (BLK, 2 * BLK), 1)
        least = jnp.where(col < BLK, from_row, col - BLK)
        score(most, extra, t, 0.0, row >= least)

        peak[...] = jnp.broadcast_to(jnp.max(peak[...], axis=1, keepdims=True), peak.shape)
        total[...] = jnp.zeros_like(total)
        weighted[...] = jnp.zeros_like(weighted)

        def weigh(c, first, second, less):
            values = jnp.concatenate([kv[g][first, :, D:], kv[g][second, :, D:]], axis=0)
            for j in range(8):
                rows = pl.ds(j * BLK, BLK)
                top = peak[rows] + less
                left = jnp.exp2(scores[c, rows, :BLK] - top)
                right = jnp.exp2(scores[c, rows, BLK:] - top)
                total[rows] += left + right
                weights = jnp.concatenate([left, right], axis=1).astype(jnp.bfloat16)
                weighted[rows] += jnp.dot(weights, values, preferred_element_type=jnp.float32)

        def two(c, carry):
            weigh(c, slots[b, 2 * c], slots[b, 2 * c + 1], biases[b, c])
            return carry

        lax.fori_loop(0, most, two, 0)
        weigh(most, extra, t, 0.0)
        for j in range(8):
            rows = pl.ds(j * BLK, BLK)
            tiles[g * 4 + i, :, j * D:(j + 1) * D] = (
                weighted[rows] / jnp.sum(total[rows], axis=1, keepdims=True)).astype(jnp.bfloat16)

    def leaving(g, i):
        cols = pl.ds(pl.multiple_of(core * 2048 + g * 1024, 1024), 1024)
        src, dst = tiles.at[g * 4 + i], out.at[(i % 2) * BLK:(i % 2 + 1) * BLK, cols]
        if i < 2:
            return pltpu.make_async_remote_copy(
                src, dst, osend.at[g * 2 + i], orecv.at[g * 2 + i], device_id=sib, device_id_type=MESH)
        return pltpu.make_async_copy(src, dst, lsem.at[9 + g * 2 + i - 2])

    def coming(g, i):
        cols = pl.ds(pl.multiple_of((1 - core) * 2048 + g * 1024, 1024), 1024)
        return pltpu.make_async_remote_copy(
            tiles.at[g * 4 + i], out.at[i * BLK:(i + 1) * BLK, cols], osend.at[g * 2 + i], orecv.at[g * 2 + i],
            device_id=sib, device_id_type=MESH)

    attend(0, 0)
    leaving(0, 0).start()
    kv_one(1)
    attend(0, 1)
    leaving(0, 1).start()
    kv_two(1)
    attend(0, 2)
    leaving(0, 2).start()
    kv_three(1)
    attend(0, 3)
    leaving(0, 3).start()
    for i in range(4):
        attend(1, i)
        leaving(1, i).start()

    def drain(at, carry):
        for kind in range(4):
            n = at * 4 + kind
            rows = pl.ds(0, 256 if kind < 2 else 128)
            ref = wbuf.at[0, 0, rows]
            pltpu.make_async_remote_copy(
                ref, ref, wsend.at[n], wrecv.at[n], device_id=xp, device_id_type=MESH).wait_send()
        return carry

    lax.fori_loop(0, 20, drain, 0)
    for g in range(2):
        kv_sent(g)
    for j in range(4):
        hidden_in(j)[1].wait_send()
    q_remote.wait_send()
    for g in range(2):
        for i in range(2):
            leaving(g, i).wait_send()
            coming(g, i).wait_recv()
            leaving(g, i + 2).wait()


def attended(slots, biases, hid, q, wk, wv, bk, bv, cos, sin):
    vmem, anywhere = pl.BlockSpec(memory_space=pltpu.VMEM), pl.BlockSpec(memory_space=pl.ANY)
    smem = pl.BlockSpec(memory_space=pltpu.SMEM)
    bf16, f32, dma = jnp.bfloat16, jnp.float32, pltpu.SemaphoreType.DMA
    return pl.pallas_call(
        whole_kernel,
        out_shape=jax.ShapeDtypeStruct((256, 4096), bf16),
        in_specs=[smem] * 2 + [anywhere] * 4 + [vmem] * 4,
        out_specs=anywhere,
        scratch_shapes=[
            pltpu.VMEM((4, 512, 2048), bf16),
            pltpu.VMEM((2, 16, 512, 256), bf16),
            pltpu.VMEM((512, 256), f32),
            pltpu.VMEM((NBLK, BLK, 2 * D), bf16),
            pltpu.VMEM((NBLK, BLK, 2 * D), bf16),
            pltpu.VMEM((512, 2048), bf16),
            pltpu.VMEM((MOST, 8 * BLK, 2 * BLK), f32),
            pltpu.VMEM((8 * BLK, BLK), f32),
            pltpu.VMEM((8 * BLK, BLK), f32),
            pltpu.VMEM((8 * BLK, D), f32),
            pltpu.VMEM((8, BLK, 8 * D), bf16),
            dma((13,)), dma((5,)), dma((5,)), dma((80,)), dma((80,)), dma((18,)), dma((18,)), dma((4,)), dma((4,)),
        ],
        compiler_params=pltpu.CompilerParams(collective_id=0, has_side_effects=True, vmem_limit_bytes=VMEM_LIMIT),
        name="attended",
    )(slots, biases, hid, q, wk, wv, bk, bv, cos, sin)


def block_table(segs, first):
    t = first + jnp.arange(4, dtype=jnp.int32)
    at = jnp.arange(NBLK, dtype=jnp.int32)
    before = at[None, :] < t[:, None]
    mine = jnp.sum(jnp.where(at[None, :] == t[:, None], segs[None, :], 0), axis=1)
    premise = jnp.sum(before & (segs == 0)[None, :], axis=1, dtype=jnp.int32)
    own = jnp.sum(before & (segs[None, :] == mine[:, None]) & (segs != 0)[None, :], axis=1, dtype=jnp.int32)
    seen = premise + own

    def block(j):
        return jnp.minimum(jnp.where(j < premise[:, None], j, j - seen[:, None] + t[:, None]), t[:, None])

    j = jnp.arange(2 * MOST, dtype=jnp.int32)[None, :]
    extra = block(jnp.maximum(seen - 1, 0)[:, None])
    from_row = jnp.where(seen % 2 == 1, -1, BLK)[:, None]
    pairs = jnp.arange(MOST, dtype=jnp.int32)[None, :]
    biases = jnp.where(2 * pairs + 1 < seen[:, None], 0.0, BIG).astype(jnp.float32)
    return jnp.concatenate([block(j), extra, from_row], axis=1).astype(jnp.int32), biases


def body(hidden_in, queries, wk, wv, bk, bv, segs):
    chip = lax.axis_index("ctx") // 2
    cos, sin = rope_tables(chip * 512, 512)
    slots, biases = block_table(segs[0], chip * 4)
    return attended(
        slots, biases, hidden_in[0], queries[0], wk, wv, bk.reshape(4, 1, D), bv.reshape(4, 1, D), cos, sin)[None]


def solution(mesh):
    placed = (P("dp", "ctx", None), P("dp", "ctx", None), P("dp", None), P("dp", None), P(), P(), P("dp", None))
    return jax.shard_map(body, mesh=mesh, in_specs=placed, out_specs=P("dp", "ctx", None), check_vma=False)
```

time: 296 us -> 145 us (0.49)
  Pallas kernels: 290 us -> 136 us
  other arithmetic: 2.01 us -> 5.83 us
    pallas_call x3 -> x1, Pallas kernels: 290 us -> 136 us  [attended(): pl.pallas_call(whole_kernel, out_shape=jax.ShapeDtypeStruct((256, 4096),...]
where the time goes in v2:
time: 145 us
  Pallas kernels  136 us (94%)
  other arithmetic  5.83 us (4%)
  local copies, waits for them, and re-layouts  3.31 us (2%)
    pallas_call x1, Pallas kernels, attended(): pl.pallas_call(whole_kernel, out_shape=jax.ShapeDtypeStruct((256, 4096),...  136 us
    unnamed x1, local copies, waits for them, and re-layouts  3.13 us

profile of v2, /device:TPU:56, one launch (start us, length us, event | category | flops | bytes accessed | tf_op | source)
XLA Modules:
  0.0 145.2 jit_solution(13495276178670676579)
XLA Ops:
  0.0 0.8 select_reduce_fusion
  0.9 0.7 compare_bitcast_fusion.1
  1.5 0.9 convert_reduce_fusion
  2.4 0.7 compare_select_fusion.1.biases
  3.1 0.1 select_minimum_fusion
  3.1 0.1 copy.11
  3.2 0.1 copy.12
  3.3 0.7 pad_add_fusion.slots
  4.0 1.0 fusion
  5.0 1.0 pad_maximum_fusion
  6.0 136.0 %attended.1 = bf16[256,4096]{1,0:T(8,128)(2,1)} custom-call(s32[4,26]{1,0:T(4,128)} %pad_add_fusion.slots, f32[4,12]{1,0:T(4,128)} %compare_select_fusion.1.biases, bf16[256,8192]{1,0:T(8,128)(2,1)} %bitcast.13, bf16[256,4096]{1,0:T(8,128)(2,1)} %bitcast.14, bf16[512,512]{1,0:T(8,128)(2,1)} %wk.1, bf16[512,512]{1,0:T(8,128)(2,1)} %wv.1, ...), custom_call_target="tpu_custom_call" | custom-call | tf_op jit(solution)/shard_map/attended/pallas_call | solution.py:428
  142.1 3.1 %copy.15 = bf16[1,256,4096]{2,1,0:T(8,128)(2,1)} copy(bf16[1,256,4096]{2,1,0:T(8,128)(2,1)} %bitcast.12) | data formatting | bytes 4194304
  (6 shorter events, 0.0 us)

commit v3 on v2

--- a/solution.py
+++ b/solution.py
@@ -1,4 +1,3 @@
-import functools
 import math
 
 import jax
@@ -30,10 +29,10 @@
 
 def whole_kernel(
     slots, biases, hid, q, wk, wv, bk, bv, cos, sin, out,
-    hbuf, wbuf, acc, kv0, kv1, q2, scores, peak, total, weighted, tiles,
+    hbuf, wbuf, acc, kv0, kv1, q2, scores0, scores1, peak0, peak1, total, weighted, tiles,
     lsem, hsend, hrecv, wsend, wrecv, ksend, krecv, osend, orecv,
 ):
-    kv = (kv0, kv1)
+    kv, scores, peaks = (kv0, kv1), (scores0, scores1), (peak0, peak1)
     dp, ctx = lax.axis_index("dp"), lax.axis_index("ctx")
     x, zh = dp // 4, dp % 4
     zl, y, core = ctx // 8, (ctx // 2) % 4, ctx % 2
@@ -301,74 +300,84 @@
     step(1, 5)
     multiply(1, ("x2", "x3", "z2", "z3"))
     kv_three(0)
-    step(1, 6)
-    multiply(1, ("x4", "z4"))
-    kv_begin(1)
 
     q_local.wait()
     others = pl.ds(pl.multiple_of((1 - core) * 256, 256), 256)
     pltpu.make_async_remote_copy(
         q.at[:, pl.ds(0, 2048)], q2.at[others], hsend.at[4], hrecv.at[4], device_id=sib, device_id_type=MESH).wait_recv()
 
-    def attend(g, i):
-        b = (i + 2 * (1 - core)) % 4
-        t = m * 4 + b
-        most = jnp.minimum(t, 2 * MOST - 1) // 2
-        q_rows = pl.ds(pl.multiple_of(b * BLK, BLK), BLK)
-
-        peak[...] = jnp.full_like(peak, -BIG)
-
-        def score(c, first, second, less, mask):
-            keys = jnp.concatenate([kv[g][first, :, :D], kv[g][second, :, :D]], axis=0)
+    pairs = jnp.minimum(m * 4 + 3, 2 * MOST - 1) // 2
+    row = lax.broadcasted_iota(jnp.int32, (BLK, 2 * BLK), 0)
+    col = lax.broadcasted_iota(jnp.int32, (BLK, 2 * BLK), 1)
+
+    def block_of(i):
+        return (i + 2 * (1 - core)) % 4
+
+    def stage(done, ahead):
+        order = lambda tile: (tile[0] * 4 + tile[1]) % 2
+        if done is not None:
+            g_done, b_done, top_ref, s_done = done[0], block_of(done[1]), peaks[order(done)], scores[order(done)]
+            top_ref[...] = jnp.broadcast_to(jnp.max(top_ref[...], axis=1, keepdims=True), top_ref.shape)
+            total[...] = jnp.zeros_like(total)
+            weighted[...] = jnp.zeros_like(weighted)
+        if ahead is not None:
+            g_ahead, b_ahead, peak_ref, s_ahead = ahead[0], block_of(ahead[1]), peaks[order(ahead)], scores[order(ahead)]
+            peak_ref[...] = jnp.full_like(peak_ref, -BIG)
+            q_rows = pl.ds(pl.multiple_of(b_ahead * BLK, BLK), BLK)
+
+        def places(b, c, last):
+            if last:
+                return slots[b, 24], m * 4 + b, 0.0
+            return slots[b, 2 * c], slots[b, 2 * c + 1], biases[b, c]
+
+        def two(c0, ends):
             for j in range(8):
                 rows = pl.ds(j * BLK, BLK)
-                s = lax.dot_general(
-                    q2[q_rows, g * 1024 + j * D:g * 1024 + (j + 1) * D], keys, (((1,), (1,)), ((), ())),
-                    preferred_element_type=jnp.float32) * SCALE
-                if mask is not None:
-                    s = jnp.where(mask, s, -BIG)
-                scores[c, rows] = s
-                top = jnp.maximum(s[:, :BLK], s[:, BLK:])
-                if mask is None:
-                    top = top - less
-                peak[rows] = jnp.maximum(peak[rows], top)
-
-        def one(c, carry):
-            score(c, slots[b, 2 * c], slots[b, 2 * c + 1], biases[b, c], None)
+                best, share, mixed = None, 0.0, 0.0
+                for u in range(2):
+                    c, last = c0 + u, ends and u == 1
+                    if ahead is not None:
+                        first, second, less = places(b_ahead, c, last)
+                        keys = jnp.concatenate([kv[g_ahead][first, :, :D], kv[g_ahead][second, :, :D]], axis=0)
+                        s = lax.dot_general(
+                            q2[q_rows, g_ahead * 1024 + j * D:g_ahead * 1024 + (j + 1) * D], keys,
+                            (((1,), (1,)), ((), ())), preferred_element_type=jnp.float32) * SCALE
+                        if last:
+                            least = jnp.where(col < BLK, slots[b_ahead, 25], col - BLK)
+                            s = jnp.where(row >= least, s, -BIG)
+                        s_ahead[c, rows] = s
+                        here = jnp.maximum(s[:, :BLK], s[:, BLK:])
+                        if not last:
+                            here = here - less
+                        best = here if best is None else jnp.maximum(best, here)
+                    if done is not None:
+                        first, second, less = places(b_done, c, last)
+                        values = jnp.concatenate([kv[g_done][first, :, D:], kv[g_done][second, :, D:]], axis=0)
+                        top = top_ref[rows] if last else top_ref[rows] + less
+                        left = jnp.exp2(s_done[c, rows, :BLK] - top)
+                        right = jnp.exp2(s_done[c, rows, BLK:] - top)
+                        share += left + right
+                        weights = jnp.concatenate([left, right], axis=1).astype(jnp.bfloat16)
+                        mixed += jnp.dot(weights, values, preferred_element_type=jnp.float32)
+                if ahead is not None:
+                    peak_ref[rows] = jnp.maximum(peak_ref[rows], best)
+                if done is not None:
+                    total[rows] += share
+                    weighted[rows] += mixed
+
+        def main(c, carry):
+            two(2 * c, False)
             return carry
 
-        lax.fori_loop(0, most, one, 0)
-        extra, from_row = slots[b, 24], slots[b, 25]
-        row = lax.broadcasted_iota(jnp.int32, (BLK, 2 * BLK), 0)
-        col = lax.broadcasted_iota(jnp.int32, (BLK, 2 * BLK), 1)
-        least = jnp.where(col < BLK, from_row, col - BLK)
-        score(most, extra, t, 0.0, row >= least)
-
-        peak[...] = jnp.broadcast_to(jnp.max(peak[...], axis=1, keepdims=True), peak.shape)
-        total[...] = jnp.zeros_like(total)
-        weighted[...] = jnp.zeros_like(weighted)
-
-        def weigh(c, first, second, less):
-            values = jnp.concatenate([kv[g][first, :, D:], kv[g][second, :, D:]], axis=0)
+        lax.fori_loop(0, (pairs - 1) // 2, main, 0)
+        two(pairs - 1, True)
+        if done is not None:
+            at = done[0] * 4 + done[1]
             for j in range(8):
                 rows = pl.ds(j * BLK, BLK)
-                top = peak[rows] + less
-                left = jnp.exp2(scores[c, rows, :BLK] - top)
-                right = jnp.exp2(scores[c, rows, BLK:] - top)
-                total[rows] += left + right
-                weights = jnp.concatenate([left, right], axis=1).astype(jnp.bfloat16)
-                weighted[rows] += jnp.dot(weights, values, preferred_element_type=jnp.float32)
-
-        def two(c, carry):
-            weigh(c, slots[b, 2 * c], slots[b, 2 * c + 1], biases[b, c])
-            return carry
-
-        lax.fori_loop(0, most, two, 0)
-        weigh(most, extra, t, 0.0)
-        for j in range(8):
-            rows = pl.ds(j * BLK, BLK)
-            tiles[g * 4 + i, :, j * D:(j + 1) * D] = (
-                weighted[rows] / jnp.sum(total[rows], axis=1, keepdims=True)).astype(jnp.bfloat16)
+                tiles[at, :, j * D:(j + 1) * D] = (
+                    weighted[rows] / jnp.sum(total[rows], axis=1, keepdims=True)).astype(jnp.bfloat16)
+            leaving(*done).start()
 
     def leaving(g, i):
         cols = pl.ds(pl.multiple_of(core * 2048 + g * 1024, 1024), 1024)
@@ -384,20 +393,20 @@
             tiles.at[g * 4 + i], out.at[i * BLK:(i + 1) * BLK, cols], osend.at[g * 2 + i], orecv.at[g * 2 + i],
             device_id=sib, device_id_type=MESH)
 
-    attend(0, 0)
-    leaving(0, 0).start()
+    step(1, 6)
+    multiply(1, ("x4", "z4"))
+    kv_begin(1)
+    stage(None, (0, 0))
+    stage((0, 0), (0, 1))
     kv_one(1)
-    attend(0, 1)
-    leaving(0, 1).start()
+    stage((0, 1), (0, 2))
     kv_two(1)
-    attend(0, 2)
-    leaving(0, 2).start()
+    stage((0, 2), (0, 3))
     kv_three(1)
-    attend(0, 3)
-    leaving(0, 3).start()
-    for i in range(4):
-        attend(1, i)
-        leaving(1, i).start()
+    stage((0, 3), (1, 0))
+    for i in range(3):
+        stage((1, i), (1, i + 1))
+    stage((1, 3), None)
 
     def drain(at, carry):
         for kind in range(4):
@@ -438,6 +447,8 @@
             pltpu.VMEM((NBLK, BLK, 2 * D), bf16),
             pltpu.VMEM((512, 2048), bf16),
             pltpu.VMEM((MOST, 8 * BLK, 2 * BLK), f32),
+            pltpu.VMEM((MOST, 8 * BLK, 2 * BLK), f32),
+            pltpu.VMEM((8 * BLK, BLK), f32),
             pltpu.VMEM((8 * BLK, BLK), f32),
             pltpu.VMEM((8 * BLK, BLK), f32),
             pltpu.VMEM((8 * BLK, D), f32),

time: 145 us -> 127 us (0.88)
  Pallas kernels: 136 us -> 118 us
    pallas_call x1, Pallas kernels: 136 us -> 118 us  [attended(): pl.pallas_call(whole_kernel, out_shape=jax.ShapeDtypeStruct((256, 4096),...]
where the time goes in v3:
time: 127 us
  Pallas kernels  118 us (93%)
  other arithmetic  5.83 us (5%)
  local copies, waits for them, and re-layouts  3.31 us (3%)
    pallas_call x1, Pallas kernels, attended(): pl.pallas_call(whole_kernel, out_shape=jax.ShapeDtypeStruct((256, 4096),...  118 us
    unnamed x1, local copies, waits for them, and re-layouts  3.13 us

profile of v3, /device:TPU:56, one launch (start us, length us, event | category | flops | bytes accessed | tf_op | source)
XLA Modules:
  0.0 127.0 jit_solution(5384012704075211420)
XLA Ops:
  0.0 0.8 select_reduce_fusion
  0.9 0.7 compare_bitcast_fusion.1
  1.5 0.9 convert_reduce_fusion
  2.4 0.7 compare_select_fusion.1.biases
  3.1 0.1 select_minimum_fusion
  3.1 0.1 copy.11
  3.2 0.1 copy.12
  3.3 0.7 pad_add_fusion.slots
  4.0 1.0 fusion
  5.0 1.0 pad_maximum_fusion
  6.0 117.8 %attended.1 = bf16[256,4096]{1,0:T(8,128)(2,1)} custom-call(s32[4,26]{1,0:T(4,128)} %pad_add_fusion.slots, f32[4,12]{1,0:T(4,128)} %compare_select_fusion.1.biases, bf16[256,8192]{1,0:T(8,128)(2,1)} %bitcast.13, bf16[256,4096]{1,0:T(8,128)(2,1)} %bitcast.14, bf16[512,512]{1,0:T(8,128)(2,1)} %wk.1, bf16[512,512]{1,0:T(8,128)(2,1)} %wv.1, ...), custom_call_target="tpu_custom_call" | custom-call | tf_op jit(solution)/shard_map/attended/pallas_call | solution.py:437
  123.8 3.1 %copy.15 = bf16[1,256,4096]{2,1,0:T(8,128)(2,1)} copy(bf16[1,256,4096]{2,1,0:T(8,128)(2,1)} %bitcast.12) | data formatting | bytes 4194304
  (6 shorter events, 0.0 us)

commit v4 on v3

--- a/solution.py
+++ b/solution.py
@@ -18,18 +18,9 @@
 VMEM_LIMIT = 56 * 1024 * 1024
 
 
-def rope_tables(first, count):
-    half = D // 2
-    frequency = ROPE_BASE ** (-(jnp.arange(half, dtype=jnp.float32) * 2.0 / D))
-    positions = (first + jnp.arange(count, dtype=jnp.int32)).astype(jnp.float32)
-    angles = positions[:, None] * frequency[None, :]
-    cos, sin = jnp.cos(angles), jnp.sin(angles)
-    return jnp.concatenate([cos, cos], axis=1), jnp.concatenate([-sin, sin], axis=1)
-
-
 def whole_kernel(
-    slots, biases, hid, q, wk, wv, bk, bv, cos, sin, out,
-    hbuf, wbuf, acc, kv0, kv1, q2, scores0, scores1, peak0, peak1, total, weighted, tiles,
+    slots, biases, hid, q, wk, wv, bk, bv, frequency, out,
+    cos, sin, hbuf, wbuf, acc, kv0, kv1, q2, scores0, scores1, peak0, peak1, total, weighted, tiles,
     lsem, hsend, hrecv, wsend, wrecv, ksend, krecv, osend, orecv,
 ):
     kv, scores, peaks = (kv0, kv1), (scores0, scores1), (peak0, peak1)
@@ -227,25 +218,25 @@
         k_send(g, zl, 1)
 
     def kv_one(g):
+        @pl.when(zl == 1)
+        def _():
+            cross(g, y).wait_recv()
+            k_send(g, 0, 0)
+            k_send(g, 0, 1)
+
         for kind in range(2):
             k_wait(g, zl, kind)
             k_send(g, zl, kind + 2)
 
-        @pl.when(zl == 1)
-        def _():
-            cross(g, y).wait_recv()
-            k_send(g, 0, 0)
-            k_send(g, 0, 1)
-
     def kv_two(g):
-        k_wait(g, zl, 2)
-        k_wait(g, zl, 3)
-
         @pl.when(zl == 1)
         def _():
             for kind in range(2):
                 k_wait(g, 0, kind)
                 k_send(g, 0, kind + 2)
+
+        k_wait(g, zl, 2)
+        k_wait(g, zl, 3)
 
     def kv_three(g):
         @pl.when(zl == 1)
@@ -275,6 +266,10 @@
     q_remote.start()
     step(0, 1)
     step(0, 2)
+    angles = (m * 512 + lax.broadcasted_iota(jnp.int32, (512, D), 0)).astype(jnp.float32) * frequency[...]
+    cos[...] = jnp.cos(angles)
+    half = lax.broadcasted_iota(jnp.int32, (512, D), 1) < D // 2
+    sin[...] = jnp.where(half, -1.0, 1.0) * jnp.sin(angles)
     step(0, 3)
     begin(1)
     step(0, 4)
@@ -430,16 +425,18 @@
             leaving(g, i + 2).wait()
 
 
-def attended(slots, biases, hid, q, wk, wv, bk, bv, cos, sin):
+def attended(slots, biases, hid, q, wk, wv, bk, bv, frequency):
     vmem, anywhere = pl.BlockSpec(memory_space=pltpu.VMEM), pl.BlockSpec(memory_space=pl.ANY)
     smem = pl.BlockSpec(memory_space=pltpu.SMEM)
     bf16, f32, dma = jnp.bfloat16, jnp.float32, pltpu.SemaphoreType.DMA
     return pl.pallas_call(
         whole_kernel,
         out_shape=jax.ShapeDtypeStruct((256, 4096), bf16),
-        in_specs=[smem] * 2 + [anywhere] * 4 + [vmem] * 4,
+        in_specs=[smem] * 2 + [anywhere] * 4 + [vmem] * 3,
         out_specs=anywhere,
         scratch_shapes=[
+            pltpu.VMEM((512, D), f32),
+            pltpu.VMEM((512, D), f32),
             pltpu.VMEM((4, 512, 2048), bf16),
             pltpu.VMEM((2, 16, 512, 256), bf16),
             pltpu.VMEM((512, 256), f32),
@@ -457,14 +454,14 @@
         ],
         compiler_params=pltpu.CompilerParams(collective_id=0, has_side_effects=True, vmem_limit_bytes=VMEM_LIMIT),
         name="attended",
-    )(slots, biases, hid, q, wk, wv, bk, bv, cos, sin)
+    )(slots, biases, hid, q, wk, wv, bk, bv, frequency)
 
 
 def block_table(segs, first):
     t = first + jnp.arange(4, dtype=jnp.int32)
     at = jnp.arange(NBLK, dtype=jnp.int32)
     before = at[None, :] < t[:, None]
-    mine = jnp.sum(jnp.where(at[None, :] == t[:, None], segs[None, :], 0), axis=1)
+    mine = lax.dynamic_slice_in_dim(segs, first, 4)
     premise = jnp.sum(before & (segs == 0)[None, :], axis=1, dtype=jnp.int32)
     own = jnp.sum(before & (segs[None, :] == mine[:, None]) & (segs != 0)[None, :], axis=1, dtype=jnp.int32)
     seen = premise + own
@@ -482,10 +479,11 @@
 
 def body(hidden_in, queries, wk, wv, bk, bv, segs):
     chip = lax.axis_index("ctx") // 2
-    cos, sin = rope_tables(chip * 512, 512)
+    frequency = ROPE_BASE ** (-(jnp.arange(D // 2, dtype=jnp.float32) * 2.0 / D))
+    frequency = jnp.concatenate([frequency, frequency])[None]
     slots, biases = block_table(segs[0], chip * 4)
     return attended(
-        slots, biases, hidden_in[0], queries[0], wk, wv, bk.reshape(4, 1, D), bv.reshape(4, 1, D), cos, sin)[None]
+        slots, biases, hidden_in[0], queries[0], wk, wv, bk.reshape(4, 1, D), bv.reshape(4, 1, D), frequency)[None]
 
 
 def solution(mesh):

time: 127 us -> 126 us (level); the launches traced: 127 us -> 125 us
  other arithmetic: 5.83 us -> 3.59 us
where the time goes in v4:
time: 126 us; the launch traced here: 125 us
  Pallas kernels  117 us (93%)
  local copies, waits for them, and re-layouts  4.04 us (3%)
  other arithmetic  3.59 us (3%)
    pallas_call x1, Pallas kernels, attended(): pl.pallas_call(whole_kernel, out_shape=jax.ShapeDtypeStruct((256, 4096),...  117 us
    unnamed x1, local copies, waits for them, and re-layouts  3.13 us

profile of v4, /device:TPU:56, one launch (start us, length us, event | category | flops | bytes accessed | tf_op | source)
XLA Modules:
  0.0 124.5 jit_solution(9385714514396277469)
XLA Ops:
  0.0 0.7 dynamic-slice_bitcast_fusion
  0.7 0.6 maximum_bitcast_fusion.frequency
  1.4 0.7 compare_bitcast_fusion.1
  2.0 0.9 convert_reduce_fusion
  2.9 0.7 compare_select_fusion.1.biases
  3.6 0.1 select_minimum_fusion
  3.7 0.1 copy.11
  3.7 0.1 copy.12
  3.9 0.7 pad_add_fusion.slots
  4.5 116.9 %attended.1 = bf16[256,4096]{1,0:T(8,128)(2,1)} custom-call(s32[4,26]{1,0:T(4,128)} %pad_add_fusion.slots, f32[4,12]{1,0:T(4,128)} %compare_select_fusion.1.biases, bf16[256,8192]{1,0:T(8,128)(2,1)} %bitcast.17, bf16[256,4096]{1,0:T(8,128)(2,1)} %bitcast.18, bf16[512,512]{1,0:T(8,128)(2,1)} %wk.1, bf16[512,512]{1,0:T(8,128)(2,1)} %wv.1, ...), custom_call_target="tpu_custom_call" | custom-call | tf_op jit(solution)/shard_map/attended/pallas_call | solution.py:432
  121.4 3.1 %copy.15 = bf16[1,256,4096]{2,1,0:T(8,128)(2,1)} copy(bf16[1,256,4096]{2,1,0:T(8,128)(2,1)} %bitcast.16) | data formatting | bytes 4194304
  (5 shorter events, 0.0 us)
